TPU v7x, 32 devices: a whole 2x2x4 slice. The times are simulated.
32 devices in a mesh: expert: 4 (over x, core), fsdp: 8 (over z, y).
Axes of the slice: x: 2, y: 2, z: 4, core: 2. Of those that a mesh axis runs over, the one named last changes fastest.
Arguments:
- tokens: bfloat16 [4096, 1536], P(('expert', 'fsdp')), may hold values from -6 to 6
- gate_probs: float32 [4096, 2], P(('expert', 'fsdp')), may hold values from 0.1 to 1
- expert_ids: int32 [4096, 2], P(('expert', 'fsdp')), may hold values from 0 to 3, all different within a row; in each aligned block of 128 rows (0 to 127, 128 to 255, ...) at most 64 rows name the same one
- cotangent: bfloat16 [4096, 1536], P(('expert', 'fsdp')), may hold values from -0.59765625 to 0.59765625
- gate_weight: bfloat16 [4, 1536, 2048], P('expert', None, 'fsdp'), may hold values from -0.15625 to 0.15625
- up_weight: bfloat16 [4, 1536, 2048], P('expert', None, 'fsdp'), may hold values from -0.15625 to 0.15625
- down_weight: bfloat16 [4, 2048, 1536], P('expert', 'fsdp'), may hold values from -0.125 to 0.125
Outputs:
- mixed: bfloat16 [4096, 1536], P(('expert', 'fsdp'))
- d_tokens: bfloat16 [4096, 1536], P(('expert', 'fsdp'))
- d_gates: float32 [4096, 2], P(('expert', 'fsdp'))
- d_gate_weight: float32 [4, 1536, 2048], P('expert', None, 'fsdp')
- d_up_weight: float32 [4, 1536, 2048], P('expert', None, 'fsdp')
- d_down_weight: float32 [4, 2048, 1536], P('expert', 'fsdp')
Inputs may be any that keep to these rules, and one draw needn't show every extreme that they name: `expert_ids`: the two experts of a token differ. In the 128 rows of one device every expert is named exactly 64 times.
All inputs are finite; a program needn't handle non-finite values.
Results may differ from a plain program's by a relative error of at most 0.015.
Values may be sent and summed in bfloat16 or wider, within the bound.
No kernel may reach another device: no remote copies, remote signals or barrier semaphores. Data moves between devices by JAX's collectives and lax.ppermute only.
A program may use at most 192 MiB of HBM per device.

v0:
```python
import jax
import jax.numpy as jnp
from jax import lax
from jax.sharding import PartitionSpec as P


def build_dispatch(expert_ids, capacity, num_experts):
    flat_ids = expert_ids.reshape(-1)
    onehot = (flat_ids[:, None] == jnp.arange(num_experts, dtype=jnp.int32)[None, :]).astype(
        jnp.int32
    )
    before = jnp.cumsum(onehot, axis=0) - onehot
    slot_pos = jnp.sum(before * onehot, axis=1)
    target = flat_ids * capacity + slot_pos
    return (jnp.arange(num_experts * capacity, dtype=jnp.int32)[:, None] == target[None, :]).astype(
        jnp.bfloat16
    )


def deliver(buffer):
    arrived = lax.all_to_all(buffer, "expert", split_axis=0, concat_axis=0, tiled=True)
    arrived = lax.all_gather(arrived[None], "fsdp", axis=0, tiled=True)
    return arrived.reshape(-1, buffer.shape[-1])


def bring_back(partial_value, num_experts, capacity):
    columns = partial_value.shape[-1]
    blocks = partial_value.astype(jnp.bfloat16).reshape(-1, num_experts, capacity, columns)
    summed = lax.psum_scatter(blocks, "fsdp", scatter_dimension=0, tiled=True).astype(jnp.float32)
    result = lax.all_to_all(
        summed[0].astype(jnp.bfloat16), "expert", split_axis=0, concat_axis=0, tiled=True
    )
    return result.reshape(num_experts * capacity, columns)


def per_device(tokens, gate_probs, expert_ids, cotangent, gate_weight, up_weight, down_weight):
    tok_rows, columns = tokens.shape
    num_experts = lax.axis_size("expert")
    capacity = 2 * tok_rows // num_experts
    dispatch = build_dispatch(expert_ids, capacity, num_experts)
    token_map = jnp.sum(dispatch.reshape(num_experts * capacity, tok_rows, 2), axis=2)
    contract_rows = (((0,), (0,)), ((), ()))
    contract_cols = (((1,), (1,)), ((), ()))
    outgoing = jnp.dot(token_map, tokens, preferred_element_type=jnp.float32).astype(jnp.bfloat16)
    cot_wide = cotangent.astype(jnp.float32)
    scaled = (
        (gate_probs[:, :, None] * cot_wide[:, None, :])
        .astype(jnp.bfloat16)
        .reshape(2 * tok_rows, columns)
    )
    grad_out = jnp.dot(dispatch, scaled, preferred_element_type=jnp.float32).astype(jnp.bfloat16)
    token_slots = outgoing.reshape(num_experts, capacity, columns)
    grad_slots = grad_out.reshape(num_experts, capacity, columns)
    rows_in = deliver(token_slots)
    w_gate = gate_weight[0]
    w_up = up_weight[0]
    w_down = down_weight[0]
    pre_gate = jnp.dot(rows_in, w_gate, preferred_element_type=jnp.float32)
    pre_up = jnp.dot(rows_in, w_up, preferred_element_type=jnp.float32)
    sigmoid_gate = jax.nn.sigmoid(pre_gate)
    hidden = (pre_gate * sigmoid_gate * pre_up).astype(jnp.bfloat16)
    partial_value = jnp.dot(hidden, w_down, preferred_element_type=jnp.float32)
    expert_out = bring_back(partial_value, num_experts, capacity)
    per_pair = lax.dot_general(
        dispatch, expert_out, contract_rows, preferred_element_type=jnp.float32
    ).reshape(tok_rows, 2, columns)
    mixed = jnp.sum(gate_probs[:, :, None] * per_pair, axis=1).astype(jnp.bfloat16)
    d_gates = jnp.sum(cot_wide[:, None, :] * per_pair, axis=2)
    grad_rows = deliver(grad_slots)
    d_hidden = lax.dot_general(grad_rows, w_down, contract_cols, preferred_element_type=jnp.float32)
    d_pre_gate = (
        d_hidden * pre_up * sigmoid_gate * (1.0 + pre_gate * (1.0 - sigmoid_gate))
    ).astype(jnp.bfloat16)
    d_pre_up = (d_hidden * pre_gate * sigmoid_gate).astype(jnp.bfloat16)
    d_down = lax.dot_general(hidden, grad_rows, contract_rows, preferred_element_type=jnp.float32)
    d_gate_w = lax.dot_general(
        rows_in, d_pre_gate, contract_rows, preferred_element_type=jnp.float32
    )
    d_up_w = lax.dot_general(rows_in, d_pre_up, contract_rows, preferred_element_type=jnp.float32)
    back_partial = lax.dot_general(
        d_pre_gate, w_gate, contract_cols, preferred_element_type=jnp.float32
    )
    back_partial = back_partial + lax.dot_general(
        d_pre_up, w_up, contract_cols, preferred_element_type=jnp.float32
    )
    d_rows = bring_back(back_partial, num_experts, capacity)
    d_tokens = lax.dot_general(
        token_map, d_rows, contract_rows, preferred_element_type=jnp.float32
    ).astype(jnp.bfloat16)
    return (mixed, d_tokens, d_gates, d_gate_w[None], d_up_w[None], d_down[None])


def solution(mesh):
    placed = (
        P(("expert", "fsdp"), None),
        P(("expert", "fsdp"), None),
        P(("expert", "fsdp"), None),
        P(("expert", "fsdp"), None),
        P("expert", None, "fsdp"),
        P("expert", None, "fsdp"),
        P("expert", "fsdp", None),
    )
    return jax.shard_map(
        per_device,
        mesh=mesh,
        in_specs=placed,
        out_specs=(
            P(("expert", "fsdp"), None),
            P(("expert", "fsdp"), None),
            P(("expert", "fsdp"), None),
            P("expert", None, "fsdp"),
            P("expert", None, "fsdp"),
            P("expert", "fsdp", None),
        ),
        check_vma=False,
    )
```

profile of v0, /device:TPU:0, one launch (start us, length us, event | category | flops | bytes accessed | tf_op | source)
XLA Modules:
  0.0 503.3 jit_solution(16064644596484839438)
XLA Ops:
  7.2 0.0 copy-start
  7.2 0.0 copy-start.9
  7.2 0.0 copy-start.1
  7.2 0.0 all-gather.5.cloned.1.call-start
  7.2 0.9 copy.44
  8.1 0.1 reshape.107
  8.3 0.1 eq.62
  8.4 1.2 reduce-window.6
  9.6 0.1 slice.8
  9.7 0.1 copy.46
  9.9 0.1 copy.47
  10.0 0.1 add_bitcast_fusion
  10.1 0.1 reduce_sum.42
  10.2 0.1 copy.48
  10.3 0.7 multiply_add_fusion
  11.0 0.0 copy-start.7
  11.0 0.6 copy-done.7
  11.6 1.3 convolution_convert_fusion.1
  13.0 15.8 %all_to_all.20 = bf16[4,64,1536]{2,1,0:T(8,128)(2,1)} all-to-all(bf16[4,64,1536]{2,1,0:T(8,128)(2,1)S(1)} %bitcast.76), channel_id=1, replica_groups=mesh['expert'=4,'fsdp'=8] {'expert'}, dimensions={0} | all-to-all | bytes 1572864 | tf_op jit(solution)/shard_map/all_to_all | solution.py:21
  28.8 0.0 all-gather.5.cloned.1.call-update
  28.8 0.0 all-gather.7.cloned.1.call-start
  28.8 0.0 copy-done.9
  28.8 0.1 copy.50
  29.0 0.1 mul.83
  29.1 0.0 copy-done.1
  29.1 1.5 mul.85.clone
  30.7 2.4 mul.86
  33.0 0.0 copy-start.5
  33.1 0.5 convolution_convert_fusion.2
  33.5 14.8 %all_to_all.21 = bf16[4,64,1536]{2,1,0:T(8,128)(2,1)} all-to-all(bf16[4,64,1536]{2,1,0:T(8,128)(2,1)S(1)} %bitcast.77), channel_id=1, replica_groups=mesh['expert'=4,'fsdp'=8] {'expert'}, dimensions={0} | all-to-all | bytes 1572864 | tf_op jit(solution)/shard_map/all_to_all | solution.py:21
  48.3 0.0 all-gather.7.cloned.1.call-update
  48.3 0.2 reduce-scatter.5.cloned.1.call-start
  48.6 80.2 %all-gather.5.cloned.1.call-done = bf16[32,64,1536]{2,1,0:T(8,128)(2,1)} async-done(((bf16[4,64,1536]{2,1,0:T(8,128)(2,1)}), bf16[32,64,1536]{2,1,0:T(8,128)(2,1)}) %all-gather.5.cloned.1.call-update) | async-done | bytes 6291472 | tf_op jit(solution)/shard_map/all_gather | solution.py:22
  128.7 6.0 %fusion.4 = f32[2048,256]{1,0:T(8,128)} fusion(bf16[2048,1536]{1,0:T(8,128)(2,1)} %bitcast.81, bf16[1,1536,256]{2,1,0:T(8,128)(2,1)S(1)} %copy-done.5), kind=kOutput, calls=%fused_computation.19 | convolution fusion | flops 1610612736 | bytes 9175040 | tf_op jit(solution)/shard_map/dot_general | solution.py:59
  134.8 0.0 copy-done.10
  134.8 3.1 fusion.8
  137.9 90.2 %all-gather.7.cloned.1.call-done = bf16[32,64,1536]{2,1,0:T(8,128)(2,1)} async-done(((bf16[4,64,1536]{2,1,0:T(8,128)(2,1)}), bf16[32,64,1536]{2,1,0:T(8,128)(2,1)}) %all-gather.7.cloned.1.call-update) | async-done | bytes 6291472 | tf_op jit(solution)/shard_map/all_gather | solution.py:22
  228.2 0.0 copy-done
  228.2 6.6 %multiply_convert_fusion = (bf16[2048,256]{1,0:T(8,128)(2,1)S(1)}, bf16[2048,256]{1,0:T(8,128)(2,1)S(1)}, bf16[2048,256]{1,0:T(8,128)(2,1)S(1)}) fusion(f32[2048,256]{1,0:T(8,128)} %fusion.8, f32[2048,256]{1,0:T(8,128)} %fusion.4, bf16[2048,1536]{1,0:T(8,128)(2,1)} %bitcast.73, bf16[1,256,1536]{2,1,0:T(8,128)(2,1)S(1)} %copy-done), kind=kOutput, calls=%fused_computation.8 | convolution fusion | flops 1619001344 | bytes 14417920 | tf_op jit(solution)/shard_map/dot_general | solution.py:70
  234.8 0.0 copy-start.2
  234.8 0.0 copy-start.6
  234.8 1.8 fusion.6
  236.6 0.0 copy-done.2
  236.7 0.0 copy-done.6
  236.7 4.6 add_convert_fusion
  241.3 0.0 reduce-scatter.5.cloned.1.call-update
  241.3 0.3 reduce-scatter.3.cloned.1.call-start
  241.6 4.4 convolution_convert_fusion
  246.0 0.0 reduce-scatter.3.cloned.1.call-update
  246.0 0.9 convert_element_type.65
  246.9 0.1 iota_compare_fusion.2
  247.0 0.1 eq.68
  247.1 5.8 %convolution_bitcast_fusion.1 = f32[1,1536,256]{2,1,0:T(8,128)} fusion(bf16[2048,1536]{1,0:T(8,128)(2,1)} %bitcast.82, bf16[2048,256]{1,0:T(8,128)(2,1)S(1)} %get-tuple-element.8), kind=kOutput, calls=%fused_computation.3 | convolution fusion | flops 1610612736 | bytes 8912896 | tf_op jit(solution)/shard_map/dot_general | solution.py:79
  252.9 104.7 %reduce-scatter.5.cloned.1.call-done = bf16[1,4,64,1536]{3,2,1,0:T(8,128)(2,1)} async-done(((bf16[8,4,64,1536]{3,2,1,0:T(8,128)(2,1)}), bf16[1,4,64,1536]{3,2,1,0:T(8,128)(2,1)}) %reduce-scatter.5.cloned.1.call-update) | async-done | bytes 786448 | tf_op jit(solution)/shard_map/reduce_scatter | solution.py:29
  357.6 3.5 all-to-all-start.3
  361.1 6.0 %convolution_bitcast_fusion.2 = f32[1,1536,256]{2,1,0:T(8,128)} fusion(bf16[2048,1536]{1,0:T(8,128)(2,1)} %bitcast.83, bf16[2048,256]{1,0:T(8,128)(2,1)} %copy-done.2), kind=kOutput, calls=%fused_computation.4 | convolution fusion | flops 1610612736 | bytes 8912896 | tf_op jit(solution)/shard_map/dot_general | solution.py:76
  367.1 111.0 %reduce-scatter.3.cloned.1.call-done = bf16[1,4,64,1536]{3,2,1,0:T(8,128)(2,1)} async-done(((bf16[8,4,64,1536]{3,2,1,0:T(8,128)(2,1)}), bf16[1,4,64,1536]{3,2,1,0:T(8,128)(2,1)}) %reduce-scatter.3.cloned.1.call-update) | async-done | bytes 786448 | tf_op jit(solution)/shard_map/reduce_scatter | solution.py:29
  478.2 0.0 all-to-all-done.3
  478.2 4.2 all-to-all-start.1
  482.4 0.0 copy-start.8
  482.4 5.8 %convolution_bitcast_fusion = f32[1,256,1536]{2,1,0:T(8,128)} fusion(bf16[2048,256]{1,0:T(8,128)(2,1)S(1)} %get-tuple-element.10, bf16[2048,1536]{1,0:T(8,128)(2,1)} %bitcast.74), kind=kOutput, calls=%fused_computation.2 | convolution fusion | flops 1610612736 | bytes 8912896 | tf_op jit(solution)/shard_map/dot_general | solution.py:75
  488.2 1.0 convolution_convert_fusion.3
  489.2 4.9 all-to-all-done.1
  494.1 2.7 multiply_reduce_fusion
  (13 shorter events, 0.1 us)
Async XLA Ops:
  7.2 221.0 %copy-start = (bf16[1,256,1536]{2,1,0:T(8,128)(2,1)S(1)}, bf16[1,256,1536]{2,1,0:T(8,128)(2,1)}, u32[]{:S(2)}) copy-start(bf16[1,256,1536]{2,1,0:T(8,128)(2,1)} %param.13) | copy-start | bytes 2359300
  7.2 21.7 %copy-start.9 = (f32[128,2]{0,1:T(2,128)S(1)}, f32[128,2]{0,1:T(2,128)}, u32[]{:S(2)}) copy-start(f32[128,2]{0,1:T(2,128)} %param.8) | copy-start | bytes 3076
  7.2 21.9 %copy-start.1 = (bf16[128,1536]{1,0:T(8,128)(2,1)S(1)}, bf16[128,1536]{1,0:T(8,128)(2,1)}, u32[]{:S(2)}) copy-start(bf16[128,1536]{1,0:T(8,128)(2,1)} %param.10) | copy-start | bytes 1179652
  7.2 121.5 %all-gather.5.cloned.1.call-start = ((), (), s32[]{:S(2)}) async-start(), calls=%async_computation.8 | async-start | bytes 7077888 | tf_op jit(solution)/shard_map/all_gather | solution.py:22
  11.0 0.6 copy-start.7
  28.8 199.4 %all-gather.7.cloned.1.call-start = ((), (), s32[]{:S(2)}) async-start(), calls=%async_computation.9 | async-start | bytes 7077888 | tf_op jit(solution)/shard_map/all_gather | solution.py:22
  33.0 95.7 %copy-start.5 = (bf16[1,1536,256]{2,1,0:T(8,128)(2,1)S(1)}, bf16[1,1536,256]{2,1,0:T(8,128)(2,1)}, u32[]{:S(2)}) copy-start(bf16[1,1536,256]{2,1,0:T(8,128)(2,1)} %param.12) | copy-start | bytes 2359300
  48.3 309.3 %reduce-scatter.5.cloned.1.call-start = ((), (), s32[]{:S(2)}) async-start(), calls=%async_computation.7 | async-start | bytes 7077888 | tf_op jit(solution)/shard_map/reduce_scatter | solution.py:29
  128.7 6.1 %copy-start.3 = (bf16[1,1536,256]{2,1,0:T(8,128)(2,1)S(1)}, bf16[1,1536,256]{2,1,0:T(8,128)(2,1)}, u32[]{:S(2)}) copy-start(bf16[1,1536,256]{2,1,0:T(8,128)(2,1)} %param.11) | copy-start | bytes 2359300
  128.7 6.1 %copy-start.10 = (bf16[32,64,1536]{2,1,0:T(8,128)(2,1)S(1)}, bf16[32,64,1536]{2,1,0:T(8,128)(2,1)}, u32[]{:S(2)}) copy-start(bf16[32,64,1536]{2,1,0:T(8,128)(2,1)} %all-gather.5.cloned.1.call-done) | copy-start | bytes 18874372
  228.2 6.6 %copy-start.4 = (bf16[1,1536,256]{2,1,0:T(8,128)(2,1)S(1)}, bf16[1,1536,256]{2,1,0:T(8,128)(2,1)}, u32[]{:S(2)}) copy-start(bf16[1,1536,256]{2,1,0:T(8,128)(2,1)} %param.11) | copy-start | bytes 2359300
  234.8 1.9 copy-start.2
  234.8 1.9 copy-start.6
  241.3 236.9 %reduce-scatter.3.cloned.1.call-start = ((), (), s32[]{:S(2)}) async-start(), calls=%async_computation.6 | async-start | bytes 7077888 | tf_op jit(solution)/shard_map/reduce_scatter | solution.py:29
  357.6 120.6 %all-to-all-start.3 = ((bf16[4,64,1536]{2,1,0:T(8,128)(2,1)}), bf16[4,64,1536]{2,1,0:T(8,128)(2,1)S(1)}, u32[]{:S(2)}, u32[]{:S(2)}) async-start(bf16[4,64,1536]{2,1,0:T(8,128)(2,1)} %bitcast.79), calls=%async_computation.5 | async-start | bytes 1572864 | tf_op jit(solution)/shard_map/all_to_all | solution.py:30
  478.2 15.9 %all-to-all-start.1 = ((bf16[4,64,1536]{2,1,0:T(8,128)(2,1)}), bf16[4,64,1536]{2,1,0:T(8,128)(2,1)}, u32[]{:S(2)}, u32[]{:S(2)}) async-start(bf16[4,64,1536]{2,1,0:T(8,128)(2,1)} %bitcast.78), calls=%async_computation.2 | async-start | bytes 1572864 | tf_op jit(solution)/shard_map/all_to_all | solution.py:30
  482.4 5.8 %copy-start.8 = (bf16[256,128]{1,0:T(8,128)(2,1)S(1)}, bf16[256,128]{1,0:T(8,128)(2,1)}, u32[]{:S(2)}) copy-start(bf16[256,128]{1,0:T(8,128)(2,1)} %copy-done.7) | copy-start | bytes 196612
Sparse Core Ops, SparseCore 0:
  28.9 99.7 all-gather.4
  130.9 97.1 all-gather.6
  241.4 116.1 reduce-scatter.4
  361.0 117.0 reduce-scatter.2
where the time goes:
time: 504 us; the launch traced here: 503 us
  waiting for transfers between devices  391 us (78%)
  matrix products  49.8 us (10%)
  blocking collectives  30.5 us (6%)
  between operations  14 us (3%)
  starting transfers between devices  8.26 us (2%)
  local copies, waits for them, and re-layouts  6.55 us (1%)
    reduce_scatter x2, waiting for transfers between devices, bring_back(): lax.psum_scatter(blocks, 'fsdp', scatter_dimension=0, tiled=True)  216 us
    all_gather x2, waiting for transfers between devices, deliver(): arrived = lax.all_gather(arrived[None], 'fsdp', axis=0, tiled=True)  170 us
    all_to_all x2, blocking collectives, deliver(): lax.all_to_all(buffer, 'expert', split_axis=0, concat_axis=0, tiled=True)  30.5 us
  transfers between devices with their start and end apart: 6, of which 5 were waited for; matrix products, arithmetic and copies ran while one was open for 8% of the time, Pallas kernels for 0%

commit v1 on v0

v1 whole, which is shorter than its diff:
```python
import jax
import jax.numpy as jnp
from jax import lax
from jax.sharding import PartitionSpec as P


def per_device(tokens, gate_probs, expert_ids, cotangent, gate_weight, up_weight, down_weight):
    tok_rows, columns = tokens.shape
    num_experts = lax.axis_size("expert")
    shard = gate_weight.shape[2]
    f32, bf16 = jnp.float32, jnp.bfloat16
    contract_rows = (((0,), (0,)), ((), ()))
    contract_cols = (((1,), (1,)), ((), ()))

    weights = jnp.concatenate([gate_weight[0].T, up_weight[0].T, down_weight[0]], axis=0)
    weights = lax.all_gather(weights, "expert", axis=0)
    onehot = (expert_ids[:, :, None] == jnp.arange(num_experts)[None, None, :]).astype(f32)
    probs = jnp.sum(gate_probs[:, :, None] * onehot, axis=1)
    toks = lax.all_gather(tokens, "fsdp", axis=0, tiled=True)
    probs = lax.all_gather(probs, "fsdp", axis=0, tiled=True)
    cots = lax.all_gather(cotangent, "fsdp", axis=0, tiled=True)

    w_gate = weights[:, :shard].reshape(-1, columns)
    w_up = weights[:, shard : 2 * shard].reshape(-1, columns)
    w_down = weights[:, 2 * shard :].reshape(-1, columns)
    rows = toks.shape[0]

    pre_gate = lax.dot_general(toks, w_gate, contract_cols, preferred_element_type=f32)
    pre_up = lax.dot_general(toks, w_up, contract_cols, preferred_element_type=f32)
    wide = jnp.broadcast_to(probs[:, :, None], (rows, num_experts, shard)).reshape(rows, -1)
    sig = jax.nn.sigmoid(pre_gate)
    hidden = pre_gate * sig * pre_up
    hidden_p = (wide * hidden).astype(bf16)
    mixed_part = jnp.dot(hidden_p, w_down, preferred_element_type=f32).astype(bf16)
    mixed = lax.psum_scatter(mixed_part, "fsdp", scatter_dimension=0, tiled=True)

    d_raw = lax.dot_general(cots, w_down, contract_cols, preferred_element_type=f32)
    gates_part = jnp.sum((hidden * d_raw).reshape(rows, num_experts, shard), axis=2)
    d_hidden = wide * d_raw
    d_pre_gate = (d_hidden * pre_up * sig * (1.0 + pre_gate * (1.0 - sig))).astype(bf16)
    d_pre_up = (d_hidden * pre_gate * sig).astype(bf16)
    back = jnp.dot(d_pre_gate, w_gate, preferred_element_type=f32)
    back = back + jnp.dot(d_pre_up, w_up, preferred_element_type=f32)
    d_tokens = lax.psum_scatter(back.astype(bf16), "fsdp", scatter_dimension=0, tiled=True)

    gates = lax.psum_scatter(gates_part, "fsdp", scatter_dimension=0, tiled=True)
    d_gates = jnp.sum(gates[:, None, :] * onehot, axis=2)

    d_gate = lax.dot_general(d_pre_gate, toks, contract_rows, preferred_element_type=f32)
    d_up = lax.dot_general(d_pre_up, toks, contract_rows, preferred_element_type=f32)
    d_down = lax.dot_general(hidden_p, cots, contract_rows, preferred_element_type=f32)
    grads = jnp.concatenate(
        [g.astype(bf16).reshape(num_experts, shard, columns) for g in (d_gate, d_up, d_down)],
        axis=1,
    )
    grads = lax.psum_scatter(grads, "expert", scatter_dimension=0, tiled=True)[0].astype(f32)
    return (
        mixed,
        d_tokens,
        d_gates,
        grads[:shard].T[None],
        grads[shard : 2 * shard].T[None],
        grads[2 * shard :][None],
    )


def solution(mesh):
    tok = P(("expert", "fsdp"), None)
    col = P("expert", None, "fsdp")
    row = P("expert", "fsdp", None)
    return jax.shard_map(
        per_device,
        mesh=mesh,
        in_specs=(tok, tok, tok, tok, col, col, row),
        out_specs=(tok, tok, tok, col, col, row),
        check_vma=False,
    )
```

time: 504 us -> 591 us (1.17)
  waiting for transfers between devices: 391 us -> 435 us
  local copies, waits for them, and re-layouts: 6.55 us -> 32.5 us
  matrix products: 49.8 us -> 64.6 us
  other arithmetic: 3.16 us -> 17.4 us
  starting transfers between devices: 8.26 us -> 0.5 us
    unnamed x4 -> x8, waiting for transfers between devices: 0.07 us -> 62.1 us
    all_to_all x2 -> x0, blocking collectives: 30.5 us -> none  [deliver(): lax.all_to_all(buffer, 'expert', split_axis=0, concat_axis=0, tiled=True)]
    all_gather x0 -> x1, blocking collectives: none -> 26.2 us  [per_device(): probs = lax.all_gather(probs, 'fsdp', axis=0, tiled=True)]
    dot_general x13 -> x9, matrix products: 49.8 us -> 64.6 us  [the longest x1 11.2 us: per_device(): lax.dot_general(cots, w_down, contract_cols, preferred_element_type=f32)]
    reduce_scatter x2 -> x3, waiting for transfers between devices: 216 us -> 203 us  [the longest x1 78.1 us: per_device(): lax.psum_scatter(back.astype(bf16), 'fsdp', scatter_dimension=0, tiled=True)]
    reshape x1 -> x3, local copies, waits for them, and re-layouts: 0.14 us -> 12.5 us  [per_device(): g.astype(bf16).reshape(num_experts, shard, columns)]
    concatenate x0 -> x2, other arithmetic: none -> 9.07 us  [the longest x1 7.54 us: per_device(): jnp.concatenate([g.astype(bf16).reshape(num_experts, shard, columns) for...]
    slice x2, local copies, waits for them, and re-layouts: 0.18 us -> 8.47 us  [the longest x1 5.93 us: per_device(): w_gate = weights[:, :shard].reshape(-1, columns)]
  transfers between devices with their start and end apart: 6 -> 7, of which waited for: 5 -> 7; matrix products, arithmetic and copies ran while one was open for 8% -> 8% of each run, Pallas kernels for 0% -> 0%
where the time goes in v1:
time: 591 us
  waiting for transfers between devices  435 us (74%)
  matrix products  64.6 us (11%)
  local copies, waits for them, and re-layouts  32.5 us (5%)
  blocking collectives  26.2 us (4%)
  other arithmetic  17.4 us (3%)
  between operations  14.2 us (2%)
    reduce_scatter x1, waiting for transfers between devices, per_device(): lax.psum_scatter(back.astype(bf16), 'fsdp', scatter_dimension=0, tiled=True)  78.1 us
    reduce_scatter x1, waiting for transfers between devices, per_device(): lax.psum_scatter(mixed_part, 'fsdp', scatter_dimension=0, tiled=True)  71 us
    all_gather x1, waiting for transfers between devices, per_device(): weights = lax.all_gather(weights, 'expert', axis=0)  65.6 us
    unnamed x8, waiting for transfers between devices  62.1 us
    all_gather x1, waiting for transfers between devices, per_device(): toks = lax.all_gather(tokens, 'fsdp', axis=0, tiled=True)  56.7 us
    reduce_scatter x1, waiting for transfers between devices, per_device(): lax.psum_scatter(grads, 'expert', scatter_dimension=0, tiled=True)[0]  54 us
    all_gather x1, waiting for transfers between devices, per_device(): cots = lax.all_gather(cotangent, 'fsdp', axis=0, tiled=True)  47.9 us
    all_gather x1, blocking collectives, per_device(): probs = lax.all_gather(probs, 'fsdp', axis=0, tiled=True)  26.2 us
  transfers between devices with their start and end apart: 7, of which 7 were waited for; matrix products, arithmetic and copies ran while one was open for 8% of the time, Pallas kernels for 0%

profile of v1, /device:TPU:0, one launch (start us, length us, event | category | flops | bytes accessed | tf_op | source)
XLA Modules:
  0.0 590.7 jit_solution(2600725476365563583)
XLA Ops:
  7.2 0.0 copy-start.6
  7.2 0.0 all-gather.9.cloned.1.call-start
  7.2 1.5 copy.43
  8.7 1.4 copy.44
  10.1 0.0 copy-done.6
  10.1 1.5 pad_maximum_fusion.1
  11.7 0.0 all-gather.9.cloned.1.call-update
  11.7 0.0 all-gather.5.cloned.1.call-start
  11.7 0.7 all-gather.5.cloned.1.call-update
  12.4 0.0 all-gather.7.cloned.1.call-start
  12.5 0.7 all-gather.7.cloned.1.call-update
  13.2 0.0 reduce-scatter.13.cloned.1.call-start
  13.2 65.6 %all-gather.9.cloned.1.call-done = bf16[3072,1536]{1,0:T(8,128)(2,1)} async-done(((bf16[768,1536]{1,0:T(8,128)(2,1)}), bf16[3072,1536]{1,0:T(8,128)(2,1)}) %all-gather.9.cloned.1.call-update) | async-done | bytes 9437200 | tf_op jit(solution)/shard_map/all_gather | solution.py:16
  78.8 5.9 %fusion.10 = (bf16[4,256,1536]{2,1,0:T(8,128)(2,1)}, bf16[4,256,1536]{2,1,0:T(8,128)(2,1)}, bf16[4,256,1536]{2,1,0:T(8,128)(2,1)S(1)}) fusion(bf16[4,768,1536]{2,1,0:T(8,128)(2,1)} %bitcast.109), kind=kLoop, calls=%fused_computation.32 | loop fusion | bytes 18874368 | tf_op jit(solution)/shard_map/slice | solution.py:23
  84.7 0.0 copy-start.1
  84.7 56.7 %all-gather.5.cloned.1.call-done = bf16[1024,1536]{1,0:T(8,128)(2,1)} async-done(((bf16[128,1536]{1,0:T(8,128)(2,1)}), bf16[1024,1536]{1,0:T(8,128)(2,1)}) %all-gather.5.cloned.1.call-update) | async-done | bytes 3145744 | tf_op jit(solution)/shard_map/all_gather | solution.py:19
  141.4 0.0 copy-start.9
  141.5 8.4 %fusion.11 = f32[1024,1024]{1,0:T(8,128)} fusion(bf16[1024,1536]{1,0:T(8,128)(2,1)} %bitcast.112, bf16[1024,1536]{1,0:T(8,128)(2,1)} %all-gather.5.cloned.1.call-done), kind=kOutput, calls=%fused_computation.33 | convolution fusion | flops 3221225472 | bytes 10485760 | tf_op jit(solution)/shard_map/dot_general | solution.py:28
  149.9 0.0 copy-done.1
  149.9 0.0 copy-done.9
  149.9 5.0 fusion.12
  154.9 47.9 %all-gather.7.cloned.1.call-done = bf16[1024,1536]{1,0:T(8,128)(2,1)} async-done(((bf16[128,1536]{1,0:T(8,128)(2,1)}), bf16[1024,1536]{1,0:T(8,128)(2,1)}) %all-gather.7.cloned.1.call-update) | async-done | bytes 3145744 | tf_op jit(solution)/shard_map/all_gather | solution.py:21
  202.7 0.0 copy-start.7
  202.8 11.2 %bitcast_reduce_fusion = (f32[1024,4]{0,1:T(4,128)S(1)}, f32[1024,1024]{1,0:T(8,128)}) fusion(f32[1024,1024]{1,0:T(8,128)} %fusion.12, f32[1024,1024]{1,0:T(8,128)} %fusion.11, bf16[1024,1536]{1,0:T(8,128)(2,1)} %bitcast.114, bf16[1024,1536]{1,0:T(8,128)(2,1)} %all-gather.7.cloned.1.call-done), kind=kOutput, calls=%fused_computation.5 | convolution fusion | flops 3228561408 | bytes 18890752 | tf_op jit(solution)/shard_map/dot_general | solution.py:37
  214.0 1.0 copy.49
  215.0 0.0 reduce-scatter.13.cloned.1.call-update
  215.0 0.0 reduce-scatter.11.cloned.1.call-start
  215.1 60.6 %reduce-scatter.13.cloned.1.call-done = f32[128,4]{1,0:T(8,128)} async-done(((f32[1024,4]{1,0:T(8,128)}), f32[128,4]{1,0:T(8,128)}) %reduce-scatter.13.cloned.1.call-update) | async-done | bytes 2064
  275.7 0.9 copy.50
  276.6 0.0 copy-done.7
  276.6 0.0 copy-done.8
  276.6 0.6 select_reduce_fusion
  277.2 26.2 %all_gather.15 = f32[1024,4]{0,1:T(4,128)S(1)} all-gather(f32[128,4]{0,1:T(4,128)S(1)} %get-tuple-element.31), channel_id=1, replica_groups=mesh['expert'=4,'fsdp'=8] {'fsdp'}, dimensions={0}, use_global_device_ids=true | all-gather | bytes 18432 | tf_op jit(solution)/shard_map/all_gather | solution.py:20
  303.3 7.4 %fusion.9 = (bf16[1024,1024]{0,1:T(8,128)(2,1)}, bf16[1024,1024]{0,1:T(8,128)(2,1)}, bf16[1024,1024]{0,1:T(8,128)(2,1)S(1)}) fusion(f32[1024,1024]{1,0:T(8,128)} %fusion.11, f32[1024,1024]{1,0:T(8,128)} %get-tuple-element.41, f32[1024,4]{0,1:T(4,128)S(1)} %all_gather.15, f32[1024,1024]{1,0:T(8,128)} %fusion.12), kind=kLoop, calls=%fused_computation.21 | loop fusion | flops 18874368 | bytes 18890752 | tf_op jit(solution)/shard_map/convert_element_type | solution.py:41
  310.8 0.0 copy-done.10
  310.8 4.8 convolution_convert_fusion
  315.6 0.0 copy-done.5
  315.6 3.2 copy.47
  318.8 7.6 %convolution_convert_fusion.2 = bf16[1024,1536]{1,0:T(8,128)(2,1)} fusion(bf16[1024,1024]{0,1:T(8,128)(2,1)} %get-tuple-element.36, bf16[1024,1536]{1,0:T(8,128)(2,1)} %all-gather.5.cloned.1.call-done), kind=kOutput, calls=%fused_computation.24 | convolution fusion | flops 3222798336 | bytes 8388608 | tf_op jit(solution)/shard_map/dot_general | solution.py:49
  326.4 4.7 copy.45
  331.0 7.6 %convolution_convert_fusion.1 = bf16[1024,1536]{1,0:T(8,128)(2,1)} fusion(bf16[1024,1024]{0,1:T(8,128)(2,1)} %get-tuple-element.35, bf16[1024,1536]{1,0:T(8,128)(2,1)} %all-gather.5.cloned.1.call-done), kind=kOutput, calls=%fused_computation.23 | convolution fusion | flops 3222798336 | bytes 8388608 | tf_op jit(solution)/shard_map/dot_general | solution.py:50
  338.6 4.7 copy.46
  343.3 7.5 %pad_maximum_fusion = bf16[4,768,1536]{1,2,0:T(8,128)(2,1)} fusion(bf16[4,256,1536]{1,2,0:T(8,128)(2,1)S(1)} %copy.47, bf16[4,256,1536]{1,2,0:T(8,128)(2,1)} %copy.46, bf16[4,256,1536]{1,2,0:T(8,128)(2,1)} %copy.45), kind=kLoop, calls=%fused_computation | loop fusion | flops 28311552 | bytes 18874368 | tf_op jit(solution)/shard_map/concatenate | solution.py:52
  350.8 0.0 reduce-scatter.11.cloned.1.call-update
  350.9 0.0 reduce-scatter.7.cloned.1.call-start
  350.9 1.8 copy-done.3
  352.7 7.0 %convolution_convert_fusion.3 = bf16[1024,1536]{1,0:T(8,128)(2,1)} fusion(bf16[1024,1024]{0,1:T(8,128)(2,1)} %copy-done.5, bf16[1024,1536]{1,0:T(8,128)(2,1)S(1)} %bitcast.115), kind=kOutput, calls=%fused_computation.25 | convolution fusion | flops 3222798336 | bytes 8388608 | tf_op jit(solution)/shard_map/dot_general | solution.py:34
  359.7 0.0 reduce-scatter.7.cloned.1.call-update
  359.8 0.0 copy-start.2
  359.8 0.3 reduce-scatter.9.cloned.1.call-start
  360.0 0.0 copy-start.4
  360.1 7.7 %fusion.13 = f32[1024,1536]{1,0:T(8,128)S(1)} fusion(bf16[1024,1024]{0,1:T(8,128)(2,1)} %get-tuple-element.36, bf16[1024,1536]{1,0:T(8,128)(2,1)} %bitcast.113), kind=kOutput, calls=%fused_computation.35 | convolution fusion | flops 3221225472 | bytes 11534336 | tf_op jit(solution)/shard_map/dot_general | solution.py:42
  367.8 0.0 copy-done.2
  367.8 0.0 copy-done.4
  367.8 5.2 add_convert_fusion
  373.0 0.0 reduce-scatter.9.cloned.1.call-update
  373.0 54.0 %reduce-scatter.11.cloned.1.call-done = bf16[1,768,1536]{1,2,0:T(8,128)(2,1)} async-done(((bf16[4,768,1536]{1,2,0:T(8,128)(2,1)}), bf16[1,768,1536]{1,2,0:T(8,128)(2,1)}) %reduce-scatter.11.cloned.1.call-update) | async-done | bytes 2359312 | tf_op jit(solution)/shard_map/reduce_scatter | solution.py:56
  427.0 2.5 slice.38
  429.5 3.0 copy.48
  432.6 0.0 copy-done
  432.6 0.4 convert_element_type.37
  432.9 1.9 slice_bitcast_fusion
  434.8 71.0 %reduce-scatter.7.cloned.1.call-done = bf16[128,1536]{1,0:T(8,128)(2,1)} async-done(((bf16[1024,1536]{1,0:T(8,128)(2,1)}), bf16[128,1536]{1,0:T(8,128)(2,1)}) %reduce-scatter.7.cloned.1.call-update) | async-done | bytes 393232 | tf_op jit(solution)/shard_map/reduce_scatter | solution.py:35
  505.8 78.1 %reduce-scatter.9.cloned.1.call-done = bf16[128,1536]{1,0:T(8,128)(2,1)} async-done(((bf16[1024,1536]{1,0:T(8,128)(2,1)}), bf16[128,1536]{1,0:T(8,128)(2,1)}) %reduce-scatter.9.cloned.1.call-update) | async-done | bytes 393232 | tf_op jit(solution)/shard_map/reduce_scatter | solution.py:44
  (5 shorter events, 0.0 us)
Async XLA Ops:
  7.2 2.9 copy-start.6
  7.2 71.6 %all-gather.9.cloned.1.call-start = ((), (), s32[]{:S(2)}) async-start(), calls=%async_computation.9 | async-start | bytes 11796480 | tf_op jit(solution)/shard_map/all_gather | solution.py:16
  11.7 129.8 %all-gather.5.cloned.1.call-start = ((), (), s32[]{:S(2)}) async-start(), calls=%async_computation.4 | async-start | bytes 3538944 | tf_op jit(solution)/shard_map/all_gather | solution.py:19
  12.4 190.3 %all-gather.7.cloned.1.call-start = ((), (), s32[]{:S(2)}) async-start(), calls=%async_computation.6 | async-start | bytes 3538944 | tf_op jit(solution)/shard_map/all_gather | solution.py:21
  13.2 262.5 %reduce-scatter.13.cloned.1.call-start = ((), (), s32[]{:S(2)}) async-start(), calls=%async_computation.10 | async-start | bytes 589824
  84.7 65.2 %copy-start.1 = (bf16[4,256,1536]{2,1,0:T(8,128)(2,1)}, bf16[4,256,1536]{2,1,0:T(8,128)(2,1)S(1)}, u32[]{:S(2)}) copy-start(bf16[4,256,1536]{2,1,0:T(8,128)(2,1)S(1)} %get-tuple-element.34) | copy-start | bytes 9437188
  141.4 8.4 %copy-start.9 = (bf16[1024,1536]{1,0:T(8,128)(2,1)S(1)}, bf16[1024,1536]{1,0:T(8,128)(2,1)}, u32[]{:S(2)}) copy-start(bf16[1024,1536]{1,0:T(8,128)(2,1)} %all-gather.5.cloned.1.call-done) | copy-start | bytes 9437188
  202.7 73.8 %copy-start.7 = (s32[128,2]{0,1:T(2,128)S(1)}, s32[128,2]{0,1:T(2,128)}, u32[]{:S(2)}) copy-start(s32[128,2]{0,1:T(2,128)} %param.9) | copy-start | bytes 3076
  202.8 73.8 %copy-start.8 = (f32[128,2]{0,1:T(2,128)S(1)}, f32[128,2]{0,1:T(2,128)}, u32[]{:S(2)}) copy-start(f32[128,2]{0,1:T(2,128)} %param.8) | copy-start | bytes 3076
  215.0 212.0 %reduce-scatter.11.cloned.1.call-start = ((), (), s32[]{:S(2)}) async-start(), calls=%async_computation.8 | async-start | bytes 11796480 | tf_op jit(solution)/shard_map/reduce_scatter | solution.py:56
  303.3 7.4 %copy-start.10 = (bf16[1024,1536]{1,0:T(8,128)(2,1)S(1)}, bf16[1024,1536]{1,0:T(8,128)(2,1)}, u32[]{:S(2)}) copy-start(bf16[1024,1536]{1,0:T(8,128)(2,1)} %all-gather.7.cloned.1.call-done) | copy-start | bytes 9437188
  310.7 4.9 copy-start.5
  350.8 1.9 copy-start.3
  350.9 154.9 %reduce-scatter.7.cloned.1.call-start = ((), (), s32[]{:S(2)}) async-start(), calls=%async_computation.5 | async-start | bytes 3538944 | tf_op jit(solution)/shard_map/reduce_scatter | solution.py:35
  359.8 8.0 %copy-start.2 = (bf16[4,256,1536]{2,1,0:T(8,128)(2,1)S(1)}, bf16[4,256,1536]{2,1,0:T(8,128)(2,1)}, u32[]{:S(2)}) copy-start(bf16[4,256,1536]{2,1,0:T(8,128)(2,1)} %copy-done.1) | copy-start | bytes 9437188
  359.8 224.1 %reduce-scatter.9.cloned.1.call-start = ((), (), s32[]{:S(2)}) async-start(), calls=%async_computation.7 | async-start | bytes 3538944 | tf_op jit(solution)/shard_map/reduce_scatter | solution.py:44
  360.0 7.8 %copy-start.4 = (bf16[1024,1024]{0,1:T(8,128)(2,1)S(1)}, bf16[1024,1024]{0,1:T(8,128)(2,1)}, u32[]{:S(2)}) copy-start(bf16[1024,1024]{0,1:T(8,128)(2,1)} %get-tuple-element.35) | copy-start | bytes 6291460
  427.0 5.6 copy-start
Sparse Core Ops, SparseCore 0:
  11.8 66.9 all-gather.8
  81.0 60.4 all-gather.4
  143.6 59.0 all-gather.6
  215.1 60.4 reduce-scatter.12
  351.0 75.9 reduce-scatter.10
  431.4 74.2 reduce-scatter.6
  510.3 73.5 reduce-scatter.8

commit v2 on v1

v2 whole, which is shorter than its diff:
```python
import functools

import jax
import jax.numpy as jnp
from jax import lax
from jax.experimental import pallas as pl
from jax.experimental.pallas import tpu as pltpu
from jax.sharding import PartitionSpec as P

F32, BF16 = jnp.float32, jnp.bfloat16
CONTRACT_COLS = (((1,), (1,)), ((), ()))
ROUTE_ROWS = 8
VMEM_LIMIT = 48 * 1024 * 1024


def hop(value, axis, step):
    return lax.ppermute(value, axis, [(i, i ^ step) for i in range(lax.axis_size(axis))])


def inner_size(size):
    inner = 1
    while inner * inner * 4 <= size:
        inner *= 2
    return inner


def after(value, *earlier):
    return lax.optimization_barrier((value,) + earlier)[0]


def nt(a, b):
    return lax.dot_general(a, b, CONTRACT_COLS, preferred_element_type=F32)


def nn(a, b):
    return jnp.dot(a, b, preferred_element_type=F32)


def block_kernel(steps, shards, rows, has_acc, with_xt, me_ref, *refs):
    refs = list(refs)
    pays = [refs.pop(0) for _ in range(shards)]
    weights = [(refs.pop(0), refs.pop(0)) for _ in steps]
    accs = [refs.pop(0) for _ in range(shards)] if has_acc else None
    outs = [refs.pop(0) for _ in range(shards)]
    dg_ref, du_ref, hpt_ref = refs.pop(0), refs.pop(0), refs.pop(0)
    xt_ref = refs.pop(0) if with_xt else None
    x_ref, c_ref, mixed_ref, back_ref = refs
    total = shards * rows
    columns = x_ref.shape[1]
    for j, pay in enumerate(pays):
        x_ref[j * rows : (j + 1) * rows, :] = pay[0:rows, :]
        c_ref[j * rows : (j + 1) * rows, :] = pay[rows : 2 * rows, :]
    eye = (
        lax.broadcasted_iota(jnp.int32, (rows, rows), 0)
        == lax.broadcasted_iota(jnp.int32, (rows, rows), 1)
    ).astype(BF16)
    routes = [pay[2 * rows : 2 * rows + ROUTE_ROWS, 0:rows] for pay in pays]
    stand = jnp.concatenate([nt(eye, route) for route in routes], axis=0)
    lying = jnp.concatenate([route.astype(F32) for route in routes], axis=1)
    gates = [jnp.zeros((1, total), F32), jnp.zeros((1, total), F32)]
    for i, (step, (gu, down)) in enumerate(zip(steps, weights)):
        e = (me_ref[0] ^ step).astype(F32)
        prob = jnp.where(stand[:, 4:5] == e, stand[:, 0:1] + stand[:, 2:3], 0.0)
        prob = prob + jnp.where(stand[:, 5:6] == e, stand[:, 1:2] + stand[:, 3:4], 0.0)
        pre_gate = nn(x_ref[...], gu[0])
        pre_up = nn(x_ref[...], gu[1])
        d_raw = nt(c_ref[...], down[...])
        sig = jax.nn.sigmoid(pre_gate)
        silu = pre_gate * sig
        hidden = silu * pre_up
        hidden_p = (prob * hidden).astype(BF16)
        product = (hidden * d_raw).astype(BF16)
        sums = nt(jnp.ones((8, product.shape[1]), BF16), product)[0:1]
        for k in range(2):
            gates[k] = gates[k] + jnp.where(lying[4 + k : 5 + k] == e, sums, 0.0)
        d_hidden = prob * d_raw
        d_gate = (d_hidden * pre_up * sig * (1.0 + pre_gate * (1.0 - sig))).astype(BF16)
        d_up = (d_hidden * silu).astype(BF16)
        dg_ref[i] = d_gate
        du_ref[i] = d_up
        hpt_ref[i] = hidden_p.T
        mixed = nn(hidden_p, down[...])
        back = nt(d_gate, gu[0]) + nt(d_up, gu[1])
        if i == 0:
            mixed_ref[...] = mixed
            back_ref[...] = back
        else:
            mixed_ref[...] += mixed
            back_ref[...] += back
    if with_xt:
        xt_ref[...] = x_ref[...].T
    for j, out in enumerate(outs):
        at = slice(j * rows, (j + 1) * rows)
        mixed, back = mixed_ref[at, :], back_ref[at, :]
        pair = jnp.concatenate([g[:, at] for g in gates] + [jnp.zeros((ROUTE_ROWS - 2, rows), F32)], axis=0)
        pair = jnp.concatenate([pair, jnp.zeros((ROUTE_ROWS, columns - rows), F32)], axis=1)
        if has_acc:
            mixed = mixed + accs[j][0:rows, :]
            back = back + accs[j][rows : 2 * rows, :]
            pair = pair + accs[j][2 * rows :, :]
        out[0:rows, :] = mixed.astype(out.dtype)
        out[rows : 2 * rows, :] = back.astype(out.dtype)
        out[2 * rows :, :] = pair.astype(out.dtype)


def block(me, steps, pays, weights, accs, rows, send_dtype, with_xt):
    shards, experts = len(pays), len(steps)
    columns = pays[0].shape[1]
    width = weights[0][1].shape[0]
    total = shards * rows
    args = list(pays) + [w for pair in weights for w in pair] + list(accs or [])
    outs = [jax.ShapeDtypeStruct(pays[0].shape, F32 if j == 0 else send_dtype) for j in range(shards)]
    outs += [jax.ShapeDtypeStruct((experts, total, width), BF16)] * 2
    outs += [jax.ShapeDtypeStruct((experts, width, total), BF16)]
    if with_xt:
        outs += [jax.ShapeDtypeStruct((columns, total), BF16)]
    vmem = pl.BlockSpec(memory_space=pltpu.VMEM)
    moved = sum(a.size * a.dtype.itemsize for a in args + outs)
    res = pl.pallas_call(
        functools.partial(block_kernel, tuple(steps), shards, rows, accs is not None, with_xt),
        out_shape=outs,
        in_specs=[pl.BlockSpec(memory_space=pltpu.SMEM)] + [vmem] * len(args),
        out_specs=[vmem] * len(outs),
        scratch_shapes=[pltpu.VMEM((total, columns), BF16)] * 2 + [pltpu.VMEM((total, columns), F32)] * 2,
        compiler_params=pltpu.CompilerParams(vmem_limit_bytes=VMEM_LIMIT),
        cost_estimate=pl.CostEstimate(
            flops=12 * total * columns * width * experts,
            bytes_accessed=moved,
            transcendentals=total * width * experts,
        ),
        name="block",
    )(me, *args)
    return res[:shards], res[shards : shards + 3], (res[-1] if with_xt else None)


def grad_kernel(blocks, shards, rows, slots, *refs):
    refs = list(refs)
    pays = [[refs.pop(0) for _ in range(shards)] for _ in range(blocks)]
    xts = [refs.pop(0) for _ in range(blocks)]
    acts = [(refs.pop(0), refs.pop(0), refs.pop(0)) for _ in range(blocks)]
    gu_out, down_out, c_ref = refs
    total = shards * rows
    for b in range(blocks):
        for j in range(shards):
            at = b * total + j * rows
            c_ref[at : at + rows, :] = pays[b][j][rows : 2 * rows, :]
    height = gu_out.shape[1]
    part = height // 2
    for h in range(0, height, part):
        gate = nn(xts[0][h : h + part, :], acts[0][0][slots[0]])
        up = nn(xts[0][h : h + part, :], acts[0][1][slots[0]])
        for b in range(1, blocks):
            gate = gate + nn(xts[b][h : h + part, :], acts[b][0][slots[b]])
            up = up + nn(xts[b][h : h + part, :], acts[b][1][slots[b]])
        gu_out[0, h : h + part, :] = gate.astype(gu_out.dtype)
        gu_out[1, h : h + part, :] = up.astype(gu_out.dtype)
    down = nn(acts[0][2][slots[0]], c_ref[0:total, :])
    for b in range(1, blocks):
        down = down + nn(acts[b][2][slots[b]], c_ref[b * total : (b + 1) * total, :])
    down_out[...] = down.astype(down_out.dtype)


def grad(pays, xts, acts, slots, rows, dtype):
    blocks, shards = len(pays), len(pays[0])
    columns = pays[0][0].shape[1]
    width = acts[0][0].shape[2]
    tokens = blocks * shards * rows
    args = [p for ps in pays for p in ps] + list(xts) + [a for act in acts for a in act]
    outs = [
        jax.ShapeDtypeStruct((2, columns, width), dtype),
        jax.ShapeDtypeStruct((width, columns), dtype),
    ]
    vmem = pl.BlockSpec(memory_space=pltpu.VMEM)
    return pl.pallas_call(
        functools.partial(grad_kernel, blocks, shards, rows, tuple(slots)),
        out_shape=outs,
        in_specs=[vmem] * len(args),
        out_specs=[vmem] * 2,
        scratch_shapes=[pltpu.VMEM((tokens, columns), BF16)],
        compiler_params=pltpu.CompilerParams(vmem_limit_bytes=VMEM_LIMIT),
        cost_estimate=pl.CostEstimate(
            flops=6 * tokens * columns * width,
            bytes_accessed=sum(a.size * a.dtype.itemsize for a in args + outs),
            transcendentals=0,
        ),
        name="grad",
    )(*args)


def per_device(tokens, gate_probs, expert_ids, cotangent, gate_weight, up_weight, down_weight):
    rows, columns = tokens.shape
    experts = lax.axis_size("expert")
    inner = inner_size(lax.axis_size("fsdp"))
    outer = lax.axis_size("fsdp") // inner
    me = lax.axis_index("expert").astype(jnp.int32).reshape(1)

    high = lax.reduce_precision(gate_probs, 8, 7)
    route = jnp.concatenate([high, gate_probs - high, expert_ids.astype(F32)], axis=1).T
    route = jnp.pad(route, ((0, ROUTE_ROWS - route.shape[0]), (0, columns - rows))).astype(BF16)
    own_pay = jnp.concatenate([tokens, cotangent, route], axis=0)

    own = (jnp.stack([gate_weight[0], up_weight[0]]), down_weight[0])
    weights = {0: own}
    for r in range(2, experts, 2):
        weights[r] = tuple(hop(w, "expert", r) for w in own)
    for r in range(0, experts, 2):
        weights[r + 1] = tuple(hop(w, "expert", 1) for w in weights[r])

    column = {0: own_pay}
    bit = outer // 2
    last = None
    while bit >= 1:
        for k in sorted(column):
            source = column[k] if last is None else after(column[k], last)
            column[k | bit] = last = hop(source, "fsdp", bit * inner)
        bit //= 2
    pays = {k: [v] + [hop(v, "fsdp", j) for j in range(1, inner)] for k, v in column.items()}

    near, far = [0, 1], list(range(2, experts))
    acts, xts, parts = {}, {}, {}
    arrival = list(column)
    early, late = arrival[:-1], arrival[-1:]
    for k in early:
        parts[k], act, xts[k] = block(
            me, near, pays[k], [weights[r] for r in near], None, rows, F32, True
        )
        acts[k] = [(act, near)]
    for k in late:
        parts[k], act, xts[k] = block(
            me, near + far, pays[k], [weights[r] for r in near + far], None, rows, BF16, True
        )
        acts[k] = [(act, near + far)]
    for k in early:
        parts[k], act, _ = block(
            me, far, pays[k], [weights[r] for r in far], parts[k], rows, BF16, False
        )
        acts[k].append((act, far))

    sums = {}
    for k in range(outer):
        sums[k] = parts[k][0]
        for j in range(1, inner):
            sums[k] = sums[k] + hop(parts[k][j], "fsdp", j).astype(F32)
    bit = 1
    while bit < outer:
        for k in reversed(range(bit, outer, 2 * bit)):
            sums[k - bit] = sums[k - bit] + hop(sums[k].astype(BF16), "fsdp", bit * inner).astype(F32)
        bit *= 2
    mixed = sums[0][:rows].astype(BF16)
    d_tokens = sums[0][rows : 2 * rows].astype(BF16)
    d_gates = sums[0][2 * rows : 2 * rows + 2, :rows].T

    order = range(outer)
    grads = {}
    for r in far[::-1] + near[::-1]:
        chosen, slots = [], []
        for k in order:
            for act, names in acts[k]:
                if r in names:
                    chosen.append(act)
                    slots.append(names.index(r))
        grads[r] = grad(
            [pays[k] for k in order], [xts[k] for k in order], chosen, slots, rows,
            BF16 if r % 2 else F32,
        )
    chip = {}
    for r in range(0, experts, 2):
        chip[r] = [a + hop(b, "expert", 1).astype(F32) for a, b in zip(grads[r], grads[r + 1])]
    final = chip[0]
    for r in range(2, experts, 2):
        final = [a + hop(b.astype(BF16), "expert", r).astype(F32) for a, b in zip(final, chip[r])]
    gu, down = final
    return mixed, d_tokens, d_gates, gu[0][None], gu[1][None], down[None]


def solution(mesh):
    tok = P(("expert", "fsdp"), None)
    col = P("expert", None, "fsdp")
    row = P("expert", "fsdp", None)
    return jax.shard_map(
        per_device,
        mesh=mesh,
        in_specs=(tok, tok, tok, tok, col, col, row),
        out_specs=(tok, tok, tok, col, col, row),
        check_vma=False,
    )
```

time: 591 us -> 264 us (0.45)
  waiting for transfers between devices: 435 us -> 127 us
  Pallas kernels: 0 us -> 88.1 us
  matrix products: 64.6 us -> 0 us
  blocking collectives: 26.2 us -> 0 us
  starting transfers between devices: 0.5 us -> 26.3 us
  local copies, waits for them, and re-layouts: 32.5 us -> 12.9 us
  between operations: 14.2 us -> 0.87 us
  other arithmetic: 17.4 us -> 7.69 us
    reduce_scatter x3 -> x0, waiting for transfers between devices: 203 us -> none  [the longest x1 78.1 us: per_device(): lax.psum_scatter(back.astype(bf16), 'fsdp', scatter_dimension=0, tiled=True)]
    all_gather x3 -> x0, waiting for transfers between devices: 170 us -> none  [the longest x1 65.6 us: per_device(): weights = lax.all_gather(weights, 'expert', axis=0)]
    ppermute x0 -> x26, waiting for transfers between devices: none -> 127 us  [hop(): lax.ppermute(value, axis, [(i, i ^ step) for i in range(lax.axis_size(axi...]
    pallas_call x0 -> x11, Pallas kernels: none -> 88.1 us  [the longest x7 57.7 us: block(): pl.pallas_call(functools.partial(block_kernel, tuple(steps), shards, rows...]
    dot_general x9 -> x0, matrix products: 64.6 us -> none  [the longest x1 11.2 us: per_device(): lax.dot_general(cots, w_down, contract_cols, preferred_element_type=f32)]
    unnamed x8 -> x0, waiting for transfers between devices: 62.1 us -> none
    ppermute x0 -> x26, starting transfers between devices: none -> 26.3 us  [hop(): lax.ppermute(value, axis, [(i, i ^ step) for i in range(lax.axis_size(axi...]
    all_gather x1 -> x0, blocking collectives: 26.2 us -> none  [per_device(): probs = lax.all_gather(probs, 'fsdp', axis=0, tiled=True)]
  transfers between devices with their start and end apart: 7 -> 26, of which waited for: 7 -> 11; matrix products, arithmetic and copies ran while one was open for 8% -> 3% of each run, Pallas kernels for 0% -> 33%
where the time goes in v2:
time: 264 us; the launch traced here: 263 us
  waiting for transfers between devices  127 us (48%)
  Pallas kernels  88.1 us (33%)
  starting transfers between devices  26.3 us (10%)
  local copies, waits for them, and re-layouts  12.9 us (5%)
  other arithmetic  7.69 us (3%)
    ppermute x26, waiting for transfers between devices, hop(): lax.ppermute(value, axis, [(i, i ^ step) for i in range(lax.axis_size(axi...  127 us
    pallas_call x7, Pallas kernels, block(): pl.pallas_call(functools.partial(block_kernel, tuple(steps), shards, rows...  57.7 us
    pallas_call x4, Pallas kernels, grad(): pl.pallas_call(functools.partial(grad_kernel, blocks, shards, rows, tuple...  30.4 us
    ppermute x26, starting transfers between devices, hop(): lax.ppermute(value, axis, [(i, i ^ step) for i in range(lax.axis_size(axi...  26.3 us
    unnamed x61, local copies, waits for them, and re-layouts  9.49 us
  transfers between devices with their start and end apart: 26, of which 11 were waited for; matrix products, arithmetic and copies ran while one was open for 3% of the time, Pallas kernels for 33%

profile of v2, /device:TPU:0, one launch (start us, length us, event | category | flops | bytes accessed | tf_op | source)
XLA Modules:
  0.0 263.2 jit_solution(2485891301659927997)
XLA Ops:
  0.7 1.3 constant_dynamic-update-slice_fusion.1
  2.0 0.1 constant_dynamic-update-slice_fusion.refs_2_
  2.1 3.0 %collective-permute-start.1 = (bf16[2,1536,256]{2,1,0:T(8,128)(2,1)S(1)}, bf16[2,1536,256]{2,1,0:T(8,128)(2,1)}, u32[]{:S(2)}, u32[]{:S(2)}) collective-permute-start(bf16[2,1536,256]{2,1,0:T(8,128)(2,1)S(1)} %constant_dynamic-update-slice_fusion.refs_2_), channel_id=1, source_target_pairs={{0,16},{8,24},{16,0},{24,8},{1,17},{9,25},{17,1},{25,9},{2,18},{10... | collective-permute-start | bytes 4718600 | tf_op jit(solution)/shard_map/ppermute | solution.py:17
  5.1 0.1 fusion.1.refs_0_
  5.2 2.7 %collective-permute-start.8 = (bf16[264,1536]{1,0:T(8,128)(2,1)S(1)}, bf16[264,1536]{1,0:T(8,128)(2,1)S(1)}, u32[]{:S(2)}, u32[]{:S(2)}) collective-permute-start(bf16[264,1536]{1,0:T(8,128)(2,1)S(1)} %fusion.1.refs_0_), channel_id=1, source_target_pairs={{0,4},{1,5},{2,6},{3,7},{4,0},{5,1},{6,2},{7,3},{8,12},{9,13},{10,... | collective-permute-start | bytes 2433032 | tf_op jit(solution)/shard_map/ppermute | solution.py:17
  7.9 0.5 collective-permute-start.5
  8.4 34.7 %collective-permute-done.8.refs_0_.refs_4_ = bf16[264,1536]{1,0:T(8,128)(2,1)S(1)} collective-permute-done((bf16[264,1536]{1,0:T(8,128)(2,1)S(1)}, bf16[264,1536]{1,0:T(8,128)(2,1)S(1)}, u32[]{:S(2)}, u32[]{:S(2)}) %collective-permute-start.8) | collective-permute-done | bytes 811040 | tf_op jit(solution)/shard_map/ppermute | solution.py:17
  43.1 0.7 collective-permute-start.9
  43.8 1.5 collective-permute-start
  45.3 0.9 copy-done.11
  46.2 0.5 collective-permute-start.2
  46.7 15.3 %collective-permute-done.9.refs_0_.refs_2_ = bf16[264,1536]{1,0:T(8,128)(2,1)S(1)} collective-permute-done((bf16[264,1536]{1,0:T(8,128)(2,1)S(1)}, bf16[264,1536]{1,0:T(8,128)(2,1)S(1)}, u32[]{:S(2)}, u32[]{:S(2)}) %collective-permute-start.9) | collective-permute-done | bytes 811040 | tf_op jit(solution)/shard_map/ppermute | solution.py:17
  62.0 1.5 collective-permute-start.13
  63.5 1.6 collective-permute-done.2.refs_3_.refs_7_
  65.2 0.3 collective-permute-start.15
  65.5 0.6 collective-permute-start.10
  66.1 1.1 copy-done.27
  67.2 1.1 copy-done.9
  68.3 1.1 copy-done.12
  69.5 7.0 %block.7 = (f32[264,1536]{1,0:T(8,128)}, f32[264,1536]{1,0:T(8,128)}, bf16[2,256,256]{2,1,0:T(8,128)(2,1)S(1)}, bf16[2,256,256]{2,1,0:T(8,128)(2,1)S(1)}, bf16[2...) custom-call(s32[1]{0:T(128)} %bitcast.me_ref, bf16[264,1536]{1,0:T(8,128)(2,1)S(1)} %fusion.1.refs_0_, ...), custom_call_target="tpu_custom_call" | custom-call | flops 2415919104 | bytes 11157504 | tf_op jit(solution)/shard_map/block/pallas_call | solution.py:119
  76.5 6.7 %collective-permute-done.13.refs_1_.refs_5_ = bf16[264,1536]{1,0:T(8,128)(2,1)} collective-permute-done((bf16[264,1536]{1,0:T(8,128)(2,1)S(1)}, bf16[264,1536]{1,0:T(8,128)(2,1)}, u32[]{:S(2)}, u32[]{:S(2)}) %collective-permute-start.13) | collective-permute-done | bytes 811040 | tf_op jit(solution)/shard_map/ppermute | solution.py:17
  83.1 7.2 %block.11 = (f32[264,1536]{1,0:T(8,128)}, f32[264,1536]{1,0:T(8,128)}, bf16[2,256,256]{2,1,0:T(8,128)(2,1)S(1)}, bf16[2,256,256]{2,1,0:T(8,128)(2,1)S(1)}, bf16[...) custom-call(s32[1]{0:T(128)} %bitcast.me_ref, bf16[264,1536]{1,0:T(8,128)(2,1)S(1)} %collective-permute-done.8.refs_0_.refs_4_, ...), custom_call_target="tpu_custom_call" | custom-call | flops 2415919104 | bytes 11157504 | tf_op jit(solution)/shard_map/block/pallas_call | solution.py:119
  90.3 1.5 collective-permute-start.16
  91.9 8.6 %collective-permute-done.10.refs_1_.refs_3_ = bf16[264,1536]{1,0:T(8,128)(2,1)} collective-permute-done((bf16[264,1536]{1,0:T(8,128)(2,1)S(1)}, bf16[264,1536]{1,0:T(8,128)(2,1)}, u32[]{:S(2)}, u32[]{:S(2)}) %collective-permute-start.10) | collective-permute-done | bytes 811040 | tf_op jit(solution)/shard_map/ppermute | solution.py:17
  100.5 7.2 %block.9 = (f32[264,1536]{1,0:T(8,128)}, f32[264,1536]{1,0:T(8,128)}, bf16[2,256,256]{2,1,0:T(8,128)(2,1)S(1)}, bf16[2,256,256]{2,1,0:T(8,128)(2,1)S(1)}, bf16[2...) custom-call(s32[1]{0:T(128)} %bitcast.me_ref, bf16[264,1536]{1,0:T(8,128)(2,1)S(1)} %collective-permute-done.9.refs_0_.refs_2_, ...), custom_call_target="tpu_custom_call" | custom-call | flops 2415919104 | bytes 11157504 | tf_op jit(solution)/shard_map/block/pallas_call | solution.py:119
  107.7 0.9 copy-done.5
  108.6 8.3 %block.12 = (f32[264,1536]{1,0:T(8,128)}, bf16[264,1536]{1,0:T(8,128)(2,1)S(1)}, bf16[2,256,256]{2,1,0:T(8,128)(2,1)S(1)}, bf16[2,256,256]{2,1,0:T(8,128)(2,1)S(1)}, bf16[2,256,256]{2,1,0:T(8,128)(2,1)S(1)}) custom-call(s32[1]{0:T(128)} %bitcast.me_ref, bf16[264,1536]{1,0:T(8,128)(2,1)S(1)} %collective-permute-done.8.refs_0_.refs_4_, ...), custom_call_target="tpu_custom_call" | custom-call | flops 2415919104 | bytes 12804096 | tf_op jit(solution)/shard_map/block/pallas_call | solution.py:119
  116.9 1.5 collective-permute-start.14
  118.4 8.4 %block.10 = (f32[264,1536]{1,0:T(8,128)}, bf16[264,1536]{1,0:T(8,128)(2,1)}, bf16[2,256,256]{2,1,0:T(8,128)(2,1)S(1)}, bf16[2,256,256]{2,1,0:T(8,128)(2,1)S(1)}, bf16[2,256,256]{2,1,0:T(8,128)(2,1)S(1)}) custom-call(s32[1]{0:T(128)} %bitcast.me_ref, bf16[264,1536]{1,0:T(8,128)(2,1)S(1)} %collective-permute-done.9.refs_0_.refs_2_, ...), custom_call_target="tpu_custom_call" | custom-call | flops 2415919104 | bytes 12804096 | tf_op jit(solution)/shard_map/block/pallas_call | solution.py:119
  126.8 0.5 collective-permute-start.11
  127.3 8.0 %block.8 = (f32[264,1536]{1,0:T(8,128)}, bf16[264,1536]{1,0:T(8,128)(2,1)S(1)}, bf16[2,256,256]{2,1,0:T(8,128)(2,1)S(1)}, bf16[2,256,256]{2,1,0:T(8,128)(2,1)S(1)}, bf16[2,256,256]{2,1,0:T(8,128)(2,1)S(1)}) custom-call(s32[1]{0:T(128)} %bitcast.me_ref, bf16[264,1536]{1,0:T(8,128)(2,1)S(1)} %fusion.1.refs_0_, ...), custom_call_target="tpu_custom_call" | custom-call | flops 2415919104 | bytes 12804096 | tf_op jit(solution)/shard_map/block/pallas_call | solution.py:119
  135.2 1.5 collective-permute-start.7
  136.8 1.1 copy-done.13
  137.9 11.8 %block.13 = (f32[264,1536]{1,0:T(8,128)}, bf16[264,1536]{1,0:T(8,128)(2,1)}, bf16[4,256,256]{2,1,0:T(8,128)(2,1)S(1)}, bf16[4,256,256]{2,1,0:T(8,128)(2,1)S(1)},...) custom-call(s32[1]{0:T(128)} %bitcast.me_ref, ...), custom_call_target="tpu_custom_call" | custom-call | flops 4831838208 | bytes 15851520 | tf_op jit(solution)/shard_map/block/pallas_call | solution.py:119
  149.7 0.9 copy-done.7
  150.5 0.5 collective-permute-start.17
  151.0 7.2 %grad.7 = (bf16[2,1536,256]{2,1,0:T(8,128)(2,1)}, bf16[256,1536]{1,0:T(8,128)(2,1)S(1)}) custom-call(bf16[264,1536]{1,0:T(8,128)(2,1)} %copy-done, bf16[264,1536]{1,0:T(8,128)(2,1)} %copy-done.3, bf16[264,1536]{1,0:T(8,128)(2,1)} %copy-done.2, bf16[264,1536]{1,0:T(8,128)(2,1)} %collective-permute-done.10.refs_1_.refs_3_, bf16[264,1536]{1,0:T(8,128)(2,1)} %copy-done.1, ...), custom_call_target="tpu_custom_call" | custom-call | flops 2415919104 | bytes 15925248 | tf_op jit(solution)/shard_map/grad/pallas_call | solution.py:174
  158.3 8.0 %grad.6 = (f32[2,1536,256]{2,1,0:T(8,128)}, f32[256,1536]{1,0:T(8,128)}) custom-call(bf16[264,1536]{1,0:T(8,128)(2,1)} %copy-done, bf16[264,1536]{1,0:T(8,128)(2,1)} %copy-done.3, bf16[264,1536]{1,0:T(8,128)(2,1)} %copy-done.2, bf16[264,1536]{1,0:T(8,128)(2,1)} %collective-permute-done.10.refs_1_.refs_3_, bf16[264,1536]{1,0:T(8,128)(2,1)} %copy-done.1, ...), custom_call_target="tpu_custom_call" | custom-call | flops 2415919104 | bytes 18284544 | tf_op jit(solution)/shard_map/grad/pallas_call | solution.py:174
  166.2 7.9 %grad.4 = (f32[2,1536,256]{2,1,0:T(8,128)}, f32[256,1536]{1,0:T(8,128)}) custom-call(bf16[264,1536]{1,0:T(8,128)(2,1)} %copy-done, bf16[264,1536]{1,0:T(8,128)(2,1)} %copy-done.3, bf16[264,1536]{1,0:T(8,128)(2,1)} %copy-done.2, bf16[264,1536]{1,0:T(8,128)(2,1)} %collective-permute-done.10.refs_1_.refs_3_, bf16[264,1536]{1,0:T(8,128)(2,1)} %copy-done.1, ...), custom_call_target="tpu_custom_call" | custom-call | flops 2415919104 | bytes 18284544 | tf_op jit(solution)/shard_map/grad/pallas_call | solution.py:174
  174.1 7.3 %grad.5 = (bf16[2,1536,256]{2,1,0:T(8,128)(2,1)}, bf16[256,1536]{1,0:T(8,128)(2,1)S(1)}) custom-call(bf16[264,1536]{1,0:T(8,128)(2,1)} %copy-done, bf16[264,1536]{1,0:T(8,128)(2,1)} %copy-done.3, bf16[264,1536]{1,0:T(8,128)(2,1)} %copy-done.2, bf16[264,1536]{1,0:T(8,128)(2,1)} %collective-permute-done.10.refs_1_.refs_3_, bf16[264,1536]{1,0:T(8,128)(2,1)} %copy-done.1, ...), custom_call_target="tpu_custom_call" | custom-call | flops 2415919104 | bytes 15925248 | tf_op jit(solution)/shard_map/grad/pallas_call | solution.py:174
  181.4 3.7 %collective-permute-done.17 = bf16[264,1536]{1,0:T(8,128)(2,1)S(1)} collective-permute-done((bf16[264,1536]{1,0:T(8,128)(2,1)}, bf16[264,1536]{1,0:T(8,128)(2,1)S(1)}, u32[]{:S(2)}, u32[]{:S(2)}) %collective-permute-start.17) | collective-permute-done | bytes 811040 | tf_op jit(solution)/shard_map/ppermute | solution.py:17
  185.1 0.2 add_convert_fusion.2
  185.4 2.3 collective-permute-start.18
  187.7 1.5 add_convert_fusion.3
  189.2 0.3 collective-permute-start.23
  189.5 0.2 add_convert_fusion.4
  189.7 1.5 collective-permute-start.12
  191.2 15.4 %collective-permute-done.18 = bf16[264,1536]{1,0:T(8,128)(2,1)S(1)} collective-permute-done((bf16[264,1536]{1,0:T(8,128)(2,1)S(1)}, bf16[264,1536]{1,0:T(8,128)(2,1)S(1)}, u32[]{:S(2)}, u32[]{:S(2)}) %collective-permute-start.18) | collective-permute-done | bytes 811040 | tf_op jit(solution)/shard_map/ppermute | solution.py:17
  206.6 0.5 collective-permute-start.25
  207.1 1.6 add_convert_fusion.1
  208.8 4.3 %collective-permute-start.19 = (bf16[264,1536]{1,0:T(8,128)(2,1)S(1)}, bf16[264,1536]{1,0:T(8,128)(2,1)S(1)}, u32[]{:S(2)}, u32[]{:S(2)}) collective-permute-start(bf16[264,1536]{1,0:T(8,128)(2,1)S(1)} %add_convert_fusion.1), channel_id=1, source_target_pairs={{0,4},{1,5},{2,6},{3,7},{4,0},{5,1},{6,2},{7,3},{8,12},{9,13},{10,... | collective-permute-start | bytes 2433032 | tf_op jit(solution)/shard_map/ppermute | solution.py:17
  213.1 0.5 add_convert_fusion
  213.6 0.9 copy-done.28
  214.5 11.3 %collective-permute-done.25 = bf16[256,1536]{1,0:T(8,128)(2,1)S(1)} collective-permute-done((bf16[256,1536]{1,0:T(8,128)(2,1)S(1)}, bf16[256,1536]{1,0:T(8,128)(2,1)S(1)}, u32[]{:S(2)}, u32[]{:S(2)}) %collective-permute-start.25) | collective-permute-done | bytes 786464 | tf_op jit(solution)/shard_map/ppermute | solution.py:17
  225.8 0.5 collective-permute-start.22
  226.3 1.4 add_bitcast_fusion
  227.7 10.4 %collective-permute-done.12 = bf16[264,1536]{1,0:T(8,128)(2,1)S(1)} collective-permute-done((bf16[264,1536]{1,0:T(8,128)(2,1)S(1)}, bf16[264,1536]{1,0:T(8,128)(2,1)S(1)}, u32[]{:S(2)}, u32[]{:S(2)}) %collective-permute-start.12) | collective-permute-done | bytes 811040 | tf_op jit(solution)/shard_map/ppermute | solution.py:17
  238.1 9.7 %collective-permute-done.19 = bf16[264,1536]{1,0:T(8,128)(2,1)S(1)} collective-permute-done((bf16[264,1536]{1,0:T(8,128)(2,1)S(1)}, bf16[264,1536]{1,0:T(8,128)(2,1)S(1)}, u32[]{:S(2)}, u32[]{:S(2)}) %collective-permute-start.19) | collective-permute-done | bytes 811040 | tf_op jit(solution)/shard_map/ppermute | solution.py:17
  247.8 1.7 fusion.3
  249.5 0.6 slice_bitcast_fusion
  250.1 0.9 fusion.5
  251.0 9.9 %collective-permute-done.22 = bf16[2,1536,256]{2,1,0:T(8,128)(2,1)S(1)} collective-permute-done((bf16[2,1536,256]{2,1,0:T(8,128)(2,1)S(1)}, bf16[2,1536,256]{2,1,0:T(8,128)(2,1)S(1)}, u32[]{:S(2)}, u32[]{:S(2)}) %collective-permute-start.22) | collective-permute-done | bytes 1572896 | tf_op jit(solution)/shard_map/ppermute | solution.py:17
  260.9 0.4 convert_add_fusion
  261.3 1.9 fusion.4
  (76 shorter events, 0.2 us)
Async XLA Ops:
  0.6 1.4 copy-start.22
  0.6 4.4 %copy-start.29 = (s32[128,2]{0,1:T(2,128)S(1)}, s32[128,2]{0,1:T(2,128)}, u32[]{:S(2)}) copy-start(s32[128,2]{0,1:T(2,128)} %param.9) | copy-start | bytes 3076
  0.7 4.4 %copy-start.26 = (f32[128,2]{0,1:T(2,128)S(1)}, f32[128,2]{0,1:T(2,128)}, u32[]{:S(2)}) copy-start(f32[128,2]{0,1:T(2,128)} %param.8) | copy-start | bytes 3076
  0.7 4.5 %copy-start.24 = (bf16[128,1536]{1,0:T(8,128)(2,1)S(1)}, bf16[128,1536]{1,0:T(8,128)(2,1)}, u32[]{:S(2)}) copy-start(bf16[128,1536]{1,0:T(8,128)(2,1)} %param.10) | copy-start | bytes 1179652
  0.7 4.5 %copy-start.25 = (bf16[128,1536]{1,0:T(8,128)(2,1)S(1)}, bf16[128,1536]{1,0:T(8,128)(2,1)}, u32[]{:S(2)}) copy-start(bf16[128,1536]{1,0:T(8,128)(2,1)} %param.7) | copy-start | bytes 1179652
  2.0 5.9 %copy-start.8 = (bf16[1,256,1536]{2,1,0:T(8,128)(2,1)S(1)}, bf16[1,256,1536]{2,1,0:T(8,128)(2,1)}, u32[]{:S(2)}) copy-start(bf16[1,256,1536]{2,1,0:T(8,128)(2,1)} %param.13) | copy-start | bytes 2359300
  2.1 63.4 %copy-start.23 = (bf16[2,1536,256]{2,1,0:T(8,128)(2,1)}, bf16[2,1536,256]{2,1,0:T(8,128)(2,1)S(1)}, u32[]{:S(2)}) copy-start(bf16[2,1536,256]{2,1,0:T(8,128)(2,1)S(1)} %constant_dynamic-update-slice_fusion.refs_2_) | copy-start | bytes 4718596
  2.1 44.6 %collective-permute-start.1 = (bf16[2,1536,256]{2,1,0:T(8,128)(2,1)S(1)}, bf16[2,1536,256]{2,1,0:T(8,128)(2,1)}, u32[]{:S(2)}, u32[]{:S(2)}) collective-permute-start(bf16[2,1536,256]{2,1,0:T(8,128)(2,1)S(1)} %constant_dynamic-update-slice_fusion.refs_2_), channel_id=1, source_target_pairs={{0,16},{8,24},{16,0},{24,8},{1,17},{9,25},{17,1},{25,9},{2,18},{10... | collective-permute-start | bytes 4718600 | tf_op jit(solution)/shard_map/ppermute | solution.py:17
  5.2 122.1 %copy-start = (bf16[264,1536]{1,0:T(8,128)(2,1)}, bf16[264,1536]{1,0:T(8,128)(2,1)S(1)}, u32[]{:S(2)}) copy-start(bf16[264,1536]{1,0:T(8,128)(2,1)S(1)} %fusion.1.refs_0_) | copy-start | bytes 2433028
  5.2 37.9 %collective-permute-start.8 = (bf16[264,1536]{1,0:T(8,128)(2,1)S(1)}, bf16[264,1536]{1,0:T(8,128)(2,1)S(1)}, u32[]{:S(2)}, u32[]{:S(2)}) collective-permute-start(bf16[264,1536]{1,0:T(8,128)(2,1)S(1)} %fusion.1.refs_0_), channel_id=1, source_target_pairs={{0,4},{1,5},{2,6},{3,7},{4,0},{5,1},{6,2},{7,3},{8,12},{9,13},{10,... | collective-permute-start | bytes 2433032 | tf_op jit(solution)/shard_map/ppermute | solution.py:17
  7.9 37.4 %collective-permute-start.6 = (bf16[256,1536]{1,0:T(8,128)(2,1)S(1)}, bf16[256,1536]{1,0:T(8,128)(2,1)S(1)}, u32[]{:S(2)}, u32[]{:S(2)}) collective-permute-start(bf16[256,1536]{1,0:T(8,128)(2,1)S(1)} %bitcast.8), channel_id=1, source_target_pairs={{0,8},{8,0},{16,24},{24,16},{1,9},{9,1},{17,25},{25,17},{2,10},{10... | collective-permute-start | bytes 2359304 | tf_op jit(solution)/shard_map/ppermute | solution.py:17
  7.9 58.2 %collective-permute-start.5 = (bf16[2,1536,256]{2,1,0:T(8,128)(2,1)S(1)}, bf16[2,1536,256]{2,1,0:T(8,128)(2,1)S(1)}, u32[]{:S(2)}, u32[]{:S(2)}) collective-permute-start(bf16[2,1536,256]{2,1,0:T(8,128)(2,1)S(1)} %constant_dynamic-update-slice_fusion.refs_2_), channel_id=1, source_target_pairs={{0,8},{8,0},{16,24},{24,16},{1,9},{9,1},{17,25},{25,17},{2,10},{10... | collective-permute-start | bytes 4718600 | tf_op jit(solution)/shard_map/ppermute | solution.py:17
  43.1 65.5 %copy-start.1 = (bf16[264,1536]{1,0:T(8,128)(2,1)}, bf16[264,1536]{1,0:T(8,128)(2,1)S(1)}, u32[]{:S(2)}) copy-start(bf16[264,1536]{1,0:T(8,128)(2,1)S(1)} %collective-permute-done.8.refs_0_.refs_4_) | copy-start | bytes 2433028
  43.1 18.9 %collective-permute-start.9 = (bf16[264,1536]{1,0:T(8,128)(2,1)S(1)}, bf16[264,1536]{1,0:T(8,128)(2,1)S(1)}, u32[]{:S(2)}, u32[]{:S(2)}) collective-permute-start(bf16[264,1536]{1,0:T(8,128)(2,1)S(1)} %fusion.1.refs_0_), channel_id=1, source_target_pairs={{0,2},{1,3},{2,0},{3,1},{4,6},{5,7},{6,4},{7,5},{8,10},{9,11},{10,... | collective-permute-start | bytes 2433032 | tf_op jit(solution)/shard_map/ppermute | solution.py:17
  43.8 21.7 %collective-permute-start = (bf16[264,1536]{1,0:T(8,128)(2,1)S(1)}, bf16[264,1536]{1,0:T(8,128)(2,1)S(1)}, u32[]{:S(2)}, u32[]{:S(2)}) collective-permute-start(bf16[264,1536]{1,0:T(8,128)(2,1)S(1)} %fusion.1.refs_0_), channel_id=1, source_target_pairs={{0,1},{1,0},{2,3},{3,2},{4,5},{5,4},{6,7},{7,6},{8,9},{9,8},{10,11... | collective-permute-start | bytes 2433032 | tf_op jit(solution)/shard_map/ppermute | solution.py:17
  45.3 0.9 copy-start.11
  46.2 19.0 %collective-permute-start.2 = (bf16[256,1536]{1,0:T(8,128)(2,1)S(1)}, bf16[256,1536]{1,0:T(8,128)(2,1)}, u32[]{:S(2)}, u32[]{:S(2)}) collective-permute-start(bf16[256,1536]{1,0:T(8,128)(2,1)S(1)} %bitcast.9), channel_id=1, source_target_pairs={{0,16},{8,24},{16,0},{24,8},{1,17},{9,25},{17,1},{25,9},{2,18},{10... | collective-permute-start | bytes 2359304 | tf_op jit(solution)/shard_map/ppermute | solution.py:17
  46.7 61.9 %collective-permute-start.3 = (bf16[2,1536,256]{2,1,0:T(8,128)(2,1)}, bf16[2,1536,256]{2,1,0:T(8,128)(2,1)}, u32[]{:S(2)}, u32[]{:S(2)}) collective-permute-start(bf16[2,1536,256]{2,1,0:T(8,128)(2,1)} %collective-permute-done.1.refs_2_.refs_6_), channel_id=1, source_target_pairs={{0,8},{8,0},{16,24},{24,16},{1,9},{9,1},{17,25},{25,17},{2,10},{10... | collective-permute-start | bytes 4718600 | tf_op jit(solution)/shard_map/ppermute | solution.py:17
  62.0 56.4 %copy-start.2 = (bf16[264,1536]{1,0:T(8,128)(2,1)}, bf16[264,1536]{1,0:T(8,128)(2,1)S(1)}, u32[]{:S(2)}) copy-start(bf16[264,1536]{1,0:T(8,128)(2,1)S(1)} %collective-permute-done.9.refs_0_.refs_2_) | copy-start | bytes 2433028
  62.0 21.1 %collective-permute-start.13 = (bf16[264,1536]{1,0:T(8,128)(2,1)S(1)}, bf16[264,1536]{1,0:T(8,128)(2,1)}, u32[]{:S(2)}, u32[]{:S(2)}) collective-permute-start(bf16[264,1536]{1,0:T(8,128)(2,1)S(1)} %collective-permute-done.8.refs_0_.refs_4_), channel_id=1, source_target_pairs={{0,1},{1,0},{2,3},{3,2},{4,5},{5,4},{6,7},{7,6},{8,9},{9,8},{10,11... | collective-permute-start | bytes 2433032 | tf_op jit(solution)/shard_map/ppermute | solution.py:17
  65.2 25.2 %collective-permute-start.15 = (bf16[264,1536]{1,0:T(8,128)(2,1)S(1)}, bf16[264,1536]{1,0:T(8,128)(2,1)}, u32[]{:S(2)}, u32[]{:S(2)}) collective-permute-start(bf16[264,1536]{1,0:T(8,128)(2,1)S(1)} %collective-permute-done.8.refs_0_.refs_4_), channel_id=1, source_target_pairs={{0,2},{1,3},{2,0},{3,1},{4,6},{5,7},{6,4},{7,5},{8,10},{9,11},{10,... | collective-permute-start | bytes 2433032 | tf_op jit(solution)/shard_map/ppermute | solution.py:17
  65.5 61.8 %copy-start.3 = (bf16[264,1536]{1,0:T(8,128)(2,1)}, bf16[264,1536]{1,0:T(8,128)(2,1)S(1)}, u32[]{:S(2)}) copy-start(bf16[264,1536]{1,0:T(8,128)(2,1)S(1)} %collective-permute-done.refs_1_) | copy-start | bytes 2433028
  65.5 35.0 %collective-permute-start.10 = (bf16[264,1536]{1,0:T(8,128)(2,1)S(1)}, bf16[264,1536]{1,0:T(8,128)(2,1)}, u32[]{:S(2)}, u32[]{:S(2)}) collective-permute-start(bf16[264,1536]{1,0:T(8,128)(2,1)S(1)} %collective-permute-done.9.refs_0_.refs_2_), channel_id=1, source_target_pairs={{0,1},{1,0},{2,3},{3,2},{4,5},{5,4},{6,7},{7,6},{8,9},{9,8},{10,11... | collective-permute-start | bytes 2433032 | tf_op jit(solution)/shard_map/ppermute | solution.py:17
  66.1 1.1 copy-start.27
  67.2 41.4 %collective-permute-start.4 = (bf16[256,1536]{1,0:T(8,128)(2,1)}, bf16[256,1536]{1,0:T(8,128)(2,1)}, u32[]{:S(2)}, u32[]{:S(2)}) collective-permute-start(bf16[256,1536]{1,0:T(8,128)(2,1)} %collective-permute-done.2.refs_3_.refs_7_), channel_id=1, source_target_pairs={{0,8},{8,0},{16,24},{24,16},{1,9},{9,1},{17,25},{25,17},{2,10},{10... | collective-permute-start | bytes 2359304 | tf_op jit(solution)/shard_map/ppermute | solution.py:17
  67.2 1.1 copy-start.9
  68.3 1.1 copy-start.12
  90.3 17.3 %copy-start.4 = (bf16[1536,256]{1,0:T(8,128)(2,1)}, bf16[1536,256]{1,0:T(8,128)(2,1)S(1)}, u32[]{:S(2)}) copy-start(bf16[1536,256]{1,0:T(8,128)(2,1)S(1)} %get-tuple-element.73.refs_10_) | copy-start | bytes 2359300
  90.3 46.4 %collective-permute-start.16 = (bf16[264,1536]{1,0:T(8,128)(2,1)}, bf16[264,1536]{1,0:T(8,128)(2,1)}, u32[]{:S(2)}, u32[]{:S(2)}) collective-permute-start(bf16[264,1536]{1,0:T(8,128)(2,1)} %collective-permute-done.15.refs_0_.refs_6_), channel_id=1, source_target_pairs={{0,1},{1,0},{2,3},{3,2},{4,5},{5,4},{6,7},{7,6},{8,9},{9,8},{10,11... | collective-permute-start | bytes 2433032 | tf_op jit(solution)/shard_map/ppermute | solution.py:17
  107.7 0.9 copy-start.5
  116.9 72.8 %collective-permute-start.14 = (bf16[264,1536]{1,0:T(8,128)(2,1)S(1)}, bf16[264,1536]{1,0:T(8,128)(2,1)}, u32[]{:S(2)}, u32[]{:S(2)}) collective-permute-start(bf16[264,1536]{1,0:T(8,128)(2,1)S(1)} %get-tuple-element.67), channel_id=1, source_target_pairs={{0,1},{1,0},{2,3},{3,2},{4,5},{5,4},{6,7},{7,6},{8,9},{9,8},{10,11... | collective-permute-start | bytes 2433032 | tf_op jit(solution)/shard_map/ppermute | solution.py:17
  126.8 58.6 %collective-permute-start.11 = (bf16[264,1536]{1,0:T(8,128)(2,1)}, bf16[264,1536]{1,0:T(8,128)(2,1)}, u32[]{:S(2)}, u32[]{:S(2)}) collective-permute-start(bf16[264,1536]{1,0:T(8,128)(2,1)} %get-tuple-element.63), channel_id=1, source_target_pairs={{0,1},{1,0},{2,3},{3,2},{4,5},{5,4},{6,7},{7,6},{8,9},{9,8},{10,11... | collective-permute-start | bytes 2433032 | tf_op jit(solution)/shard_map/ppermute | solution.py:17
  127.3 9.5 %copy-start.10 = (bf16[1,256,1536]{2,1,0:T(8,128)(2,1)S(1)}, bf16[1,256,1536]{2,1,0:T(8,128)(2,1)}, u32[]{:S(2)}) copy-start(bf16[1,256,1536]{2,1,0:T(8,128)(2,1)} %param.13) | copy-start | bytes 2359300
  135.2 92.5 %collective-permute-start.7 = (bf16[264,1536]{1,0:T(8,128)(2,1)S(1)}, bf16[264,1536]{1,0:T(8,128)(2,1)}, u32[]{:S(2)}, u32[]{:S(2)}) collective-permute-start(bf16[264,1536]{1,0:T(8,128)(2,1)S(1)} %get-tuple-element.58), channel_id=1, source_target_pairs={{0,1},{1,0},{2,3},{3,2},{4,5},{5,4},{6,7},{7,6},{8,9},{9,8},{10,11... | collective-permute-start | bytes 2433032 | tf_op jit(solution)/shard_map/ppermute | solution.py:17
  136.8 1.1 copy-start.13
  149.7 0.9 copy-start.7
  150.5 34.6 %collective-permute-start.17 = (bf16[264,1536]{1,0:T(8,128)(2,1)}, bf16[264,1536]{1,0:T(8,128)(2,1)S(1)}, u32[]{:S(2)}, u32[]{:S(2)}) collective-permute-start(bf16[264,1536]{1,0:T(8,128)(2,1)} %get-tuple-element.70), channel_id=1, source_target_pairs={{0,1},{1,0},{2,3},{3,2},{4,5},{5,4},{6,7},{7,6},{8,9},{9,8},{10,11... | collective-permute-start | bytes 2433032 | tf_op jit(solution)/shard_map/ppermute | solution.py:17
  151.0 7.2 %copy-start.6 = (bf16[1536,256]{1,0:T(8,128)(2,1)S(1)}, bf16[1536,256]{1,0:T(8,128)(2,1)}, u32[]{:S(2)}) copy-start(bf16[1536,256]{1,0:T(8,128)(2,1)} %copy-done.5) | copy-start | bytes 2359300
  158.2 50.5 %collective-permute-start.21 = (bf16[2,1536,256]{2,1,0:T(8,128)(2,1)}, bf16[2,1536,256]{2,1,0:T(8,128)(2,1)S(1)}, u32[]{:S(2)}, u32[]{:S(2)}) collective-permute-start(bf16[2,1536,256]{2,1,0:T(8,128)(2,1)} %get-tuple-element.99), channel_id=1, source_target_pairs={{0,8},{8,0},{16,24},{24,16},{1,9},{9,1},{17,25},{25,17},{2,10},{10... | collective-permute-start | bytes 4718600 | tf_op jit(solution)/shard_map/ppermute | solution.py:17
  174.1 11.0 %copy-start.18 = (f32[264,1536]{1,0:T(8,128)S(1)}, f32[264,1536]{1,0:T(8,128)}, u32[]{:S(2)}) copy-start(f32[264,1536]{1,0:T(8,128)} %get-tuple-element.69) | copy-start | bytes 4866052
  185.1 4.0 %collective-permute-start.24 = (bf16[256,1536]{1,0:T(8,128)(2,1)S(1)}, bf16[256,1536]{1,0:T(8,128)(2,1)S(1)}, u32[]{:S(2)}, u32[]{:S(2)}) collective-permute-start(bf16[256,1536]{1,0:T(8,128)(2,1)S(1)} %get-tuple-element.103), channel_id=1, source_target_pairs={{0,8},{8,0},{16,24},{24,16},{1,9},{9,1},{17,25},{25,17},{2,10},{10... | collective-permute-start | bytes 2359304 | tf_op jit(solution)/shard_map/ppermute | solution.py:17
  185.1 2.5 copy-start.17
  185.4 21.2 %collective-permute-start.18 = (bf16[264,1536]{1,0:T(8,128)(2,1)S(1)}, bf16[264,1536]{1,0:T(8,128)(2,1)S(1)}, u32[]{:S(2)}, u32[]{:S(2)}) collective-permute-start(bf16[264,1536]{1,0:T(8,128)(2,1)S(1)} %add_convert_fusion.2), channel_id=1, source_target_pairs={{0,2},{1,3},{2,0},{3,1},{4,6},{5,7},{6,4},{7,5},{8,10},{9,11},{10,... | collective-permute-start | bytes 2433032 | tf_op jit(solution)/shard_map/ppermute | solution.py:17
  187.7 1.8 copy-start.20
  189.2 18.0 %copy-start.19 = (f32[264,1536]{1,0:T(8,128)S(1)}, f32[264,1536]{1,0:T(8,128)}, u32[]{:S(2)}) copy-start(f32[264,1536]{1,0:T(8,128)} %get-tuple-element.66) | copy-start | bytes 4866052
  189.2 24.4 %collective-permute-start.23 = (bf16[256,1536]{1,0:T(8,128)(2,1)S(1)}, bf16[256,1536]{1,0:T(8,128)(2,1)S(1)}, u32[]{:S(2)}, u32[]{:S(2)}) collective-permute-start(bf16[256,1536]{1,0:T(8,128)(2,1)S(1)} %get-tuple-element.101), channel_id=1, source_target_pairs={{0,8},{8,0},{16,24},{24,16},{1,9},{9,1},{17,25},{25,17},{2,10},{10... | collective-permute-start | bytes 2359304 | tf_op jit(solution)/shard_map/ppermute | solution.py:17
  189.7 48.4 %collective-permute-start.12 = (bf16[264,1536]{1,0:T(8,128)(2,1)S(1)}, bf16[264,1536]{1,0:T(8,128)(2,1)S(1)}, u32[]{:S(2)}, u32[]{:S(2)}) collective-permute-start(bf16[264,1536]{1,0:T(8,128)(2,1)S(1)} %add_convert_fusion.3), channel_id=1, source_target_pairs={{0,2},{1,3},{2,0},{3,1},{4,6},{5,7},{6,4},{7,5},{8,10},{9,11},{10,... | collective-permute-start | bytes 2433032 | tf_op jit(solution)/shard_map/ppermute | solution.py:17
  206.6 19.2 %collective-permute-start.25 = (bf16[256,1536]{1,0:T(8,128)(2,1)S(1)}, bf16[256,1536]{1,0:T(8,128)(2,1)S(1)}, u32[]{:S(2)}, u32[]{:S(2)}) collective-permute-start(bf16[256,1536]{1,0:T(8,128)(2,1)S(1)} %add_convert_fusion.4), channel_id=1, source_target_pairs={{0,16},{8,24},{16,0},{24,8},{1,17},{9,25},{17,1},{25,9},{2,18},{10... | collective-permute-start | bytes 2359304 | tf_op jit(solution)/shard_map/ppermute | solution.py:17
  207.1 5.9 %copy-start.14 = (f32[2,1536,256]{2,1,0:T(8,128)S(1)}, f32[2,1536,256]{2,1,0:T(8,128)}, u32[]{:S(2)}) copy-start(f32[2,1536,256]{2,1,0:T(8,128)} %get-tuple-element.98) | copy-start | bytes 9437188
  208.8 39.0 %collective-permute-start.19 = (bf16[264,1536]{1,0:T(8,128)(2,1)S(1)}, bf16[264,1536]{1,0:T(8,128)(2,1)S(1)}, u32[]{:S(2)}, u32[]{:S(2)}) collective-permute-start(bf16[264,1536]{1,0:T(8,128)(2,1)S(1)} %add_convert_fusion.1), channel_id=1, source_target_pairs={{0,4},{1,5},{2,6},{3,7},{4,0},{5,1},{6,2},{7,3},{8,12},{9,13},{10,... | collective-permute-start | bytes 2433032 | tf_op jit(solution)/shard_map/ppermute | solution.py:17
  213.1 1.4 copy-start.28
  213.1 13.2 %copy-start.21 = (f32[256,1536]{1,0:T(8,128)S(1)}, f32[256,1536]{1,0:T(8,128)}, u32[]{:S(2)}) copy-start(f32[256,1536]{1,0:T(8,128)} %get-tuple-element.100) | copy-start | bytes 4718596
  214.5 36.5 %collective-permute-start.20 = (bf16[2,1536,256]{2,1,0:T(8,128)(2,1)S(1)}, bf16[2,1536,256]{2,1,0:T(8,128)(2,1)S(1)}, u32[]{:S(2)}, u32[]{:S(2)}) collective-permute-start(bf16[2,1536,256]{2,1,0:T(8,128)(2,1)S(1)} %copy-done.28), channel_id=1, source_target_pairs={{0,8},{8,0},{16,24},{24,16},{1,9},{9,1},{17,25},{25,17},{2,10},{10... | collective-permute-start | bytes 4718600 | tf_op jit(solution)/shard_map/ppermute | solution.py:17
  225.8 35.1 %collective-permute-start.22 = (bf16[2,1536,256]{2,1,0:T(8,128)(2,1)S(1)}, bf16[2,1536,256]{2,1,0:T(8,128)(2,1)S(1)}, u32[]{:S(2)}, u32[]{:S(2)}) collective-permute-start(bf16[2,1536,256]{2,1,0:T(8,128)(2,1)S(1)} %add_convert_fusion), channel_id=1, source_target_pairs={{0,16},{8,24},{16,0},{24,8},{1,17},{9,25},{17,1},{25,9},{2,18},{10... | collective-permute-start | bytes 4718600 | tf_op jit(solution)/shard_map/ppermute | solution.py:17
  226.3 21.5 %copy-start.16 = (f32[264,1536]{1,0:T(8,128)S(1)}, f32[264,1536]{1,0:T(8,128)}, u32[]{:S(2)}) copy-start(f32[264,1536]{1,0:T(8,128)} %get-tuple-element.57) | copy-start | bytes 4866052
  247.8 13.1 %copy-start.15 = (f32[2,1536,256]{2,1,0:T(8,128)S(1)}, f32[2,1536,256]{2,1,0:T(8,128)}, u32[]{:S(2)}) copy-start(f32[2,1536,256]{2,1,0:T(8,128)} %get-tuple-element.87) | copy-start | bytes 9437188
